TPU v7x, 128 devices: a whole 4x4x4 slice. The times are simulated.
128 devices in a mesh: seq: 8 (over z, core), tp: 16 (over x, y).
Axes of the slice: x: 4, y: 4, z: 4, core: 2. Of those that a mesh axis runs over, the one named last changes fastest.
Arguments:
- temporal: bfloat16 [12288, 4096], P('seq', 'tp'), may hold values from -6 to 6
- w_in: bfloat16 [4096, 1024], P('tp'), may hold values from -0.09375 to 0.09375
- audio_mask: int32 [12288], P('seq'), may hold values from 0 to 1, as said below
- counts: int32 [128], replicated, may hold values from 8 to 88, as said below
- codes: int32 [12288, 8], P(('seq', 'tp')), may hold values from 0 to 2047
- cotangent: bfloat16 [12288, 8, 1024], P(('seq', 'tp')), may hold values from -1.5 to 1.5
- norm_gain: float32 [1024], replicated, may hold values from 0.5 to 1.5
- w_qkv: bfloat16 [1024, 3072], replicated, may hold values from -8 to 8
- w_out: bfloat16 [1024, 1024], replicated, may hold values from -0.1875 to 0.1875
- adapter_a: bfloat16 [8, 2048, 128], replicated, may hold values from -6 to 6
- adapter_b: bfloat16 [8, 128, 1024], replicated, may hold values from -0.5 to 0.5
Outputs:
- grad_temporal: bfloat16 [12288, 4096], P('seq', 'tp')
- grad_w_in: float32 [4096, 1024], P('tp', 'seq')
- grad_norm_gain: float32 [1024], P(('seq', 'tp'))
- grad_w_qkv: float32 [1024, 3072], P(('seq', 'tp'))
- grad_w_out: float32 [1024, 1024], P(('seq', 'tp'))
- grad_adapter_a: float32 [8, 2048, 128], P(None, ('seq', 'tp'))
- grad_adapter_b: float32 [8, 128, 1024], P(None, ('seq', 'tp'))
Inputs may be any that keep to these rules, and one draw needn't show every extreme that they name: In every block of 96 frames the ones of audio_mask number counts of that block. counts[b] is the number of audio frames among frames b * 96 to (b + 1) * 96 - 1; for s < 8 and t < 8 the blocks s * 16 + t and s * 16 + t + 8 hold 96 audio frames together; some block holds exactly 88.
All inputs are finite; a program needn't handle non-finite values.
Results may differ from a plain program's by a relative error of at most 0.012.
The roundings to bfloat16 on the way count: a program that leaves them out, or rounds other values in their place, can miss the bound.
Values may be sent and summed in bfloat16 or wider, within the bound.
No kernel may reach another device: no remote copies, remote signals or barrier semaphores. Data moves between devices by JAX's collectives and lax.ppermute only.
A program may use at most 128 MiB of HBM per device.

v0:
```python
import math

import jax
import jax.numpy as jnp
from jax import lax
from jax.sharding import PartitionSpec as P

HEADS = 16
AUDIO = 48
PEAK = 88


def attention_backward(proj, low, upstream, weight, norm_gain, w_qkv, w_out, adapter_b):
    number = proj.shape[0]
    width = proj.shape[1]
    books = low.shape[1]
    heads = HEADS
    head_size = width // heads
    embedded = jnp.einsum("rkc,kcd->rkd", low, adapter_b, preferred_element_type=jnp.float32)
    stream = proj.astype(jnp.float32)[:, None, :] + embedded
    inv_rms = lax.rsqrt(jnp.mean(stream * stream, axis=-1, keepdims=True) + 1e-05)
    normed = (stream * inv_rms * norm_gain).astype(jnp.bfloat16)
    flat = normed.reshape(number * books, width)
    packed = jnp.dot(flat, w_qkv, preferred_element_type=jnp.float32).astype(jnp.bfloat16)
    packed = packed.reshape(number, books, 3, heads, head_size)
    query = packed[:, :, 0]
    keys = packed[:, :, 1]
    values = packed[:, :, 2]
    scale = 1.0 / math.sqrt(head_size)
    scores = jnp.einsum("rqhe,rkhe->rhqk", query, keys, preferred_element_type=jnp.float32) * scale
    causal = jnp.arange(books)[:, None] >= jnp.arange(books)[None, :]
    scores = jnp.where(causal, scores, -1e30)
    probs = jax.nn.softmax(scores, axis=-1)
    probs_low = probs.astype(jnp.bfloat16)
    mixed = jnp.einsum("rhqk,rkhe->rqhe", probs_low, values, preferred_element_type=jnp.float32)
    mixed = mixed.astype(jnp.bfloat16).reshape(number * books, width)
    grad_out = upstream.astype(jnp.float32) * weight[:, None, None]
    grad_low = grad_out.astype(jnp.bfloat16).reshape(number * books, width)
    grad_wout = jnp.einsum("nd,ne->de", mixed, grad_low, preferred_element_type=jnp.float32)
    grad_mixed = jnp.einsum("ne,de->nd", grad_low, w_out, preferred_element_type=jnp.float32)
    grad_mixed = grad_mixed.astype(jnp.bfloat16).reshape(number, books, heads, head_size)
    grad_probs = jnp.einsum(
        "rqhe,rkhe->rhqk", grad_mixed, values, preferred_element_type=jnp.float32
    )
    grad_values = jnp.einsum(
        "rhqk,rqhe->rkhe", probs_low, grad_mixed, preferred_element_type=jnp.float32
    ).astype(jnp.bfloat16)
    inner = jnp.sum(probs * grad_probs, axis=-1, keepdims=True)
    grad_scores = (probs * (grad_probs - inner) * scale).astype(jnp.bfloat16)
    grad_query = jnp.einsum(
        "rhqk,rkhe->rqhe", grad_scores, keys, preferred_element_type=jnp.float32
    ).astype(jnp.bfloat16)
    grad_keys = jnp.einsum(
        "rhqk,rqhe->rkhe", grad_scores, query, preferred_element_type=jnp.float32
    ).astype(jnp.bfloat16)
    grad_packed = jnp.stack([grad_query, grad_keys, grad_values], axis=2).reshape(
        number * books, 3 * width
    )
    grad_wqkv = jnp.einsum("nd,nf->df", flat, grad_packed, preferred_element_type=jnp.float32)
    grad_normed = jnp.einsum("nf,df->nd", grad_packed, w_qkv, preferred_element_type=jnp.float32)
    grad_normed = grad_normed.reshape(number, books, width)
    grad_gain = jnp.sum(grad_normed * stream * inv_rms, axis=(0, 1))
    scaled = grad_normed * norm_gain
    grad_stream = grad_out + inv_rms * (
        scaled - stream * inv_rms * inv_rms * jnp.mean(scaled * stream, axis=-1, keepdims=True)
    )
    return (grad_stream, (grad_gain, grad_wqkv, grad_wout))


def adapter_backward(grad_stream, low, adapter_b):
    grad_proj = jnp.sum(grad_stream, axis=1).astype(jnp.bfloat16)
    stream_low = grad_stream.astype(jnp.bfloat16)
    grad_b = jnp.einsum("rkc,rkd->kcd", low, stream_low, preferred_element_type=jnp.float32)
    grad_lowrank = jnp.einsum(
        "rkd,kcd->rkc", stream_low, adapter_b, preferred_element_type=jnp.float32
    ).astype(jnp.bfloat16)
    return (grad_proj, grad_lowrank, grad_b)


def lookup(tokens, adapter_a):
    vocab = adapter_a.shape[1]
    onehot = (tokens[:, :, None] == jnp.arange(vocab, dtype=jnp.int32)[None, None, :]).astype(
        jnp.bfloat16
    )
    low = jnp.einsum("rkv,kvc->rkc", onehot, adapter_a, preferred_element_type=jnp.float32).astype(
        jnp.bfloat16
    )
    return (onehot, low)


def compact(row):
    return jnp.nonzero(row, size=PEAK, fill_value=0)[0].astype(jnp.int32)


def local(
    temporal,
    w_in,
    audio_mask,
    counts,
    codes,
    cotangent,
    norm_gain,
    w_qkv,
    w_out,
    adapter_a,
    adapter_b,
):
    groups = lax.axis_size("tp")
    block = codes.shape[0]
    width = w_in.shape[1]
    column = lax.axis_index("tp")
    first_block = lax.axis_index("seq") * groups
    own_count = counts[first_block + column]
    mask_rows = audio_mask.reshape(groups, block)
    own_pos = compact(lax.dynamic_index_in_dim(mask_rows, column, 0, keepdims=False))
    onehot, low_own = lookup(codes[own_pos], adapter_a)
    cot_own = cotangent[own_pos]
    proj_block = lax.psum_scatter(
        jnp.dot(temporal, w_in, preferred_element_type=jnp.float32),
        "tp",
        scatter_dimension=0,
        tiled=True,
    ).astype(jnp.bfloat16)
    proj_own = proj_block[own_pos]
    valid = jnp.arange(PEAK) < own_count
    weight = jnp.where(valid, AUDIO / own_count.astype(jnp.float32), 0.0)
    grad_stream, grads = attention_backward(
        proj_own, low_own, cot_own, weight, norm_gain, w_qkv, w_out, adapter_b
    )
    grad_proj, grad_lowrank, grad_b = adapter_backward(grad_stream, low_own, adapter_b)
    own_grad_proj = jnp.where(valid[:, None], grad_proj, 0)
    own_grad_low = jnp.where(valid[:, None, None], grad_lowrank, 0)
    grad_block = jnp.zeros((block, width), jnp.bfloat16).at[own_pos].add(own_grad_proj)
    piece = lax.all_gather(grad_block, "tp", axis=0, tiled=True)
    weight_sum = jnp.einsum("nf,nd->fd", temporal, piece, preferred_element_type=jnp.float32)
    part = jnp.einsum("nd,fd->nf", piece, w_in, preferred_element_type=jnp.float32)
    grad_a = jnp.einsum("rkv,rkc->kvc", onehot, own_grad_low, preferred_element_type=jnp.float32)
    grad_win = lax.psum_scatter(weight_sum, "seq", scatter_dimension=1, tiled=True)
    grad_gain, grad_wqkv, grad_wout, grad_a, grad_b = (
        lax.psum_scatter(grads[0], ("seq", "tp"), scatter_dimension=0, tiled=True),
        lax.psum_scatter(grads[1], ("seq", "tp"), scatter_dimension=0, tiled=True),
        lax.psum_scatter(grads[2], ("seq", "tp"), scatter_dimension=0, tiled=True),
        lax.psum_scatter(grad_a, ("seq", "tp"), scatter_dimension=1, tiled=True),
        lax.psum_scatter(grad_b, ("seq", "tp"), scatter_dimension=1, tiled=True),
    )
    return (part.astype(jnp.bfloat16), grad_win, grad_gain, grad_wqkv, grad_wout, grad_a, grad_b)


def solution(mesh):
    placed = (
        P("seq", "tp"),
        P("tp", None),
        P("seq"),
        P(),
        P(("seq", "tp"), None),
        P(("seq", "tp"), None, None),
        P(),
        P(),
        P(),
        P(),
        P(),
    )
    return jax.shard_map(
        local,
        mesh=mesh,
        in_specs=placed,
        out_specs=(
            P("seq", "tp"),
            P("tp", "seq"),
            P(("seq", "tp")),
            P(("seq", "tp"), None),
            P(("seq", "tp"), None),
            P(None, ("seq", "tp"), None),
            P(None, ("seq", "tp"), None),
        ),
        check_vma=False,
    )
```

profile of v0, /device:TPU:2, one launch (start us, length us, event | category | flops | bytes accessed | tf_op | source)
XLA Modules:
  0.0 2445.6 jit_solution(8188274741854717047)
XLA Ops:
  7.2 5.1 fusion.71
  13.4 1.2 scatter_custom_fusion
  19.7 2.1 gather_fusion
  22.7 1.3 copy-done.23
  23.9 3.8 convolution_convert_fusion.2
  27.7 4.7 reshape.190
  32.4 1.2 iota_compare_fusion.9
  33.6 3.5 fusion.45
  37.1 58.7 %reduce-scatter.7.cloned.1.call-done = f32[96,1024]{1,0:T(8,128)} async-done(((f32[1536,1024]{1,0:T(8,128)}), f32[96,1024]{1,0:T(8,128)}) %reduce-scatter.7.cloned.1.call-update) | async-done | bytes 393232 | tf_op jit(solution)/shard_map/reduce_scatter | solution.py:118
  95.7 1.0 convert_element_type.130
  98.3 1.6 copy-done.1
  100.3 1.1 copy-done.13
  101.4 10.3 convolution_convert_fusion
  111.8 11.5 reshape.189
  123.3 5.2 fusion.69
  128.6 1.5 copy-done.3
  131.1 1.6 fusion.21
  132.7 5.9 fusion.70
  138.6 4.1 fusion.24
  142.7 12.2 multiply_convert_fusion
  154.9 4.2 convert_bitcast_fusion.3
  159.3 1.6 convert_bitcast_fusion.2
  161.1 4.3 convert_bitcast_fusion.1
  165.4 4.5 pad_maximum_fusion
  169.9 13.6 copy.67
  183.5 12.6 fusion.14
  196.2 5.2 fusion.68
  201.4 2.5 scatter_custom_fusion.1
  204.0 46.8 %all-gather.2.cloned.1.call-done = bf16[1536,1024]{1,0:T(8,128)(2,1)} async-done(((bf16[96,1024]{1,0:T(8,128)(2,1)}), bf16[1536,1024]{1,0:T(8,128)(2,1)}) %all-gather.2.cloned.1.call-update) | async-done | bytes 3145744 | tf_op jit(solution)/shard_map/all_gather | solution.py:134
  250.8 4.1 convolution_bitcast_fusion
  255.0 1.7 fusion.46
  256.6 4.5 copy.73
  261.2 4.8 convert_bitcast_fusion
  266.0 2.5 copy.71
  268.5 4.8 reshape.192
  273.3 5.8 fusion.31
  279.1 9.6 copy.69
  288.8 12.0 reshape.191
  300.8 10.5 fusion.33
  312.0 4.8 fusion.5
  316.8 65.0 %all-reduce = f32[1024]{0:T(1024)S(1)} all-reduce(f32[1024]{0:T(1024)S(1)} %get-tuple-element.28), channel_id=4, replica_groups=mesh['seq'=8,'tp'=16] {'seq','tp'}, use_global_device_ids=true, to_apply=%region_14.15.clone | all-reduce | flops 1024 | bytes 8192
  382.4 3.8 convolution_convert_fusion.1
  386.2 1.7 copy.74
  387.9 534.8 %reduce-scatter.17.cloned.1.call-done = f32[8,1,1024]{2,0,1:T(8,128)} async-done(((f32[8,128,1024]{2,0,1:T(8,128)}), f32[8,1,1024]{2,0,1:T(8,128)}) %reduce-scatter.17.cloned.1.call-update) | async-done | bytes 32784 | tf_op jit(solution)/shard_map/reduce_scatter | solution.py:144
  922.6 1.4 copy.75
  924.0 638.9 %reduce-scatter.13.cloned.1.call-done = f32[8,1024]{1,0:T(8,128)} async-done(((f32[1024,1024]{1,0:T(8,128)}), f32[8,1024]{1,0:T(8,128)}) %reduce-scatter.13.cloned.1.call-update) | async-done | bytes 32784 | tf_op jit(solution)/shard_map/reduce_scatter | solution.py:142
  1563.0 228.8 %reduce-scatter.11.cloned.1.call-done = f32[8,3072]{1,0:T(8,128)} async-done(((f32[1024,3072]{1,0:T(8,128)}), f32[8,3072]{1,0:T(8,128)}) %reduce-scatter.11.cloned.1.call-update) | async-done | bytes 98320 | tf_op jit(solution)/shard_map/reduce_scatter | solution.py:141
  1791.7 646.6 %reduce-scatter.15.cloned.1.call-done = f32[8,16,128]{2,1,0:T(8,128)} async-done(((f32[8,2048,128]{2,1,0:T(8,128)}), f32[8,16,128]{2,1,0:T(8,128)}) %reduce-scatter.15.cloned.1.call-update) | async-done | bytes 65552 | tf_op jit(solution)/shard_map/reduce_scatter | solution.py:143
  (90 shorter events, 11.1 us)
Async XLA Ops:
  7.2 90.4 %copy-start = (bf16[8,128,1024]{2,1,0:T(8,128)(2,1)S(1)}, bf16[8,128,1024]{2,1,0:T(8,128)(2,1)}, u32[]{:S(2)}) copy-start(bf16[8,128,1024]{2,1,0:T(8,128)(2,1)} %param.21) | copy-start | bytes 6291460
  7.2 88.5 %reduce-scatter.7.cloned.1.call-start = ((), (), s32[]{:S(2)}) async-start(), calls=%async_computation.6 | async-start | bytes 6684672 | tf_op jit(solution)/shard_map/reduce_scatter | solution.py:118
  12.3 0.7 copy-start.17
  12.3 2.6 copy-start.18
  12.3 4.8 copy-start.24
  12.3 238.5 %all-gather.2.cloned.1.call-start = ((), (), s32[]{:S(2)}) async-start(), calls=%async_computation.7 | async-start | bytes 3342336 | tf_op jit(solution)/shard_map/all_gather | solution.py:134
  16.4 3.2 copy-start.22
  19.0 0.5 copy-start.20
  21.8 5.9 copy-start.6
  21.8 2.1 copy-start.23
  37.1 61.2 %copy-start.14 = (bf16[88,8,128]{2,0,1:T(8,128)(2,1)}, bf16[88,8,128]{2,0,1:T(8,128)(2,1)S(1)}, u32[]{:S(2)}) copy-start(bf16[88,8,128]{2,0,1:T(8,128)(2,1)S(1)} %fusion.45) | copy-start | bytes 540676
  97.6 85.9 %copy-start.12 = (f32[88,1024]{1,0:T(8,128)}, f32[88,1024]{1,0:T(8,128)S(1)}, u32[]{:S(2)}) copy-start(f32[88,1024]{1,0:T(8,128)S(1)} %convert_element_type.131) | copy-start | bytes 1081348
  97.6 2.3 copy-start.16
  98.3 1.6 copy-start.1
  100.3 1.1 copy-start.13
  128.5 1.6 copy-start.3
  128.5 2.5 copy-start.5
  128.5 10.0 copy-start.11
  132.7 5.9 copy-start.9
  138.6 4.1 copy-start.25
  154.9 4.3 copy-start.4
  154.9 4.4 copy-start.8
  159.3 1.8 copy-start.10
  183.5 12.7 copy-start.2
  183.5 12.7 copy-start.7
  183.5 12.7 copy-start.21
  203.9 182.3 %reduce-scatter.9.cloned.1.call-start = ((), (), s32[]{:S(2)}) async-start(), calls=%async_computation.8 | async-start | bytes 1179648 | tf_op jit(solution)/shard_map/reduce_scatter | solution.py:138
  254.9 667.7 %reduce-scatter.17.cloned.1.call-start = ((), (), s32[]{:S(2)}) async-start(), calls=%async_computation.12 | async-start | bytes 4227072 | tf_op jit(solution)/shard_map/reduce_scatter | solution.py:144
  261.1 1301.8 %reduce-scatter.13.cloned.1.call-start = ((), (), s32[]{:S(2)}) async-start(), calls=%async_computation.10 | async-start | bytes 4227072 | tf_op jit(solution)/shard_map/reduce_scatter | solution.py:142
  279.1 1512.6 %reduce-scatter.11.cloned.1.call-start = ((), (), s32[]{:S(2)}) async-start(), calls=%async_computation.9 | async-start | bytes 12681216 | tf_op jit(solution)/shard_map/reduce_scatter | solution.py:141
  311.3 0.7 copy-start.19
  311.3 2127.0 %reduce-scatter.15.cloned.1.call-start = ((), (), s32[]{:S(2)}) async-start(), calls=%async_computation.11 | async-start | bytes 8454144 | tf_op jit(solution)/shard_map/reduce_scatter | solution.py:143
  316.7 65.7 %copy-start.15 = (bf16[256,1024]{1,0:T(8,128)(2,1)S(1)}, bf16[256,1024]{1,0:T(8,128)(2,1)}, u32[]{:S(2)}) copy-start(bf16[256,1024]{1,0:T(8,128)(2,1)} %param.12) | copy-start | bytes 1572868
Sparse Core Ops, SparseCore 0:
  12.4 83.2 reduce-scatter.6
  204.1 46.6 all-gather.1
  255.0 31.7 reduce-scatter.8
  289.1 633.4 reduce-scatter.16
  925.5 637.4 reduce-scatter.12
  1568.4 223.3 reduce-scatter.10
  1794.7 643.5 reduce-scatter.14
where the time goes:
time: 2470 us; the launch traced here: 2450 us
  waiting for transfers between devices  2150 us (87%)
  matrix products  87.3 us (4%)
  local copies, waits for them, and re-layouts  85.3 us (3%)
  blocking collectives  65 us (3%)
  other arithmetic  37.4 us (2%)
    reduce_scatter x1, waiting for transfers between devices, local(): lax.psum_scatter(grad_a, ('seq', 'tp'), scatter_dimension=1, tiled=True)  647 us
    reduce_scatter x1, waiting for transfers between devices, local(): lax.psum_scatter(grads[2], ('seq', 'tp'), scatter_dimension=0, tiled=True)  639 us
    reduce_scatter x1, waiting for transfers between devices, local(): lax.psum_scatter(grad_b, ('seq', 'tp'), scatter_dimension=1, tiled=True)  535 us
    reduce_scatter x1, waiting for transfers between devices, local(): lax.psum_scatter(grads[1], ('seq', 'tp'), scatter_dimension=0, tiled=True)  229 us
    unnamed x1, blocking collectives  65 us
    reduce_scatter x1, waiting for transfers between devices, local(): lax.psum_scatter(jnp.dot(temporal, w_in, preferred_element_type=jnp.float...  58.7 us
  transfers between devices with their start and end apart: 7, of which 6 were waited for; matrix products, arithmetic and copies ran while one was open for 4% of the time, Pallas kernels for 0%

commit v1 on v0

v1 whole, which is shorter than its diff:
```python
import math

import jax
import jax.numpy as jnp
from jax import lax
from jax.experimental import pallas as pl
from jax.experimental.pallas import tpu as pltpu
from jax.sharding import Mesh, PartitionSpec as P

HEADS = 16
AUDIO = 48
EXTRA = 40
BLOCK = 96
BOOKS = 8
RANK = 128
GROUP = 16
GROUPS = AUDIO // GROUP
ROWS = AUDIO * BOOKS
SPAN = GROUP * BOOKS
TPS = 16
WIDTH = 1024
VOCAB = 2048
LEFT = 3 * WIDTH
GAIN = 128
RIGHT = 5 * WIDTH + GAIN - LEFT
TABLE = VOCAB
F32 = jnp.float32
BF16 = jnp.bfloat16
I32 = jnp.int32
NT = (((1,), (1,)), ((), ()))
TN = (((0,), (0,)), ((), ()))
MIB = 1024 * 1024


def dot(a, b, dims=None):
    if dims is None:
        return jnp.dot(a, b, preferred_element_type=F32)
    return lax.dot_general(a, b, dims, preferred_element_type=F32)


def iota(shape, dim):
    return lax.broadcasted_iota(I32, shape, dim)


def ones_where(cond):
    return jnp.where(cond, 1.0, 0.0).astype(BF16)


def shaped(*shape, dtype=BF16):
    return jax.ShapeDtypeStruct(shape, dtype)


def call(kernel, name, out, args, scalars=0, scratch=(), limit=12):
    vmem = pl.BlockSpec(memory_space=pltpu.VMEM)
    smem = pl.BlockSpec(memory_space=pltpu.SMEM)
    return pl.pallas_call(
        kernel,
        out_shape=out,
        in_specs=[smem] * scalars + [vmem] * (len(args) - scalars),
        out_specs=jax.tree.map(lambda _: vmem, out),
        scratch_shapes=list(scratch),
        compiler_params=pltpu.CompilerParams(vmem_limit_bytes=limit * MIB),
        cost_estimate=pl.CostEstimate(flops=0, bytes_accessed=0, transcendentals=0),
        name=name,
    )(*args)


def ranks(mask_ref):
    mask = mask_ref[...].astype(F32)
    before = ones_where(iota((BLOCK, BLOCK), 0) < iota((BLOCK, BLOCK), 1))
    rank = dot(mask.astype(BF16), before)
    return mask > 0, rank, jnp.sum(mask, axis=1, keepdims=True)


def own_row(a, column):
    a = jnp.broadcast_to(a, (TPS, a.shape[1]))
    return jnp.sum(jnp.where(iota(a.shape, 0) == column, a, 0.0), axis=0, keepdims=True)


def each_book(row):
    spread = ones_where(iota((BLOCK, BLOCK * BOOKS), 1) // BOOKS == iota((BLOCK, BLOCK * BOOKS), 0))
    wide = dot(jnp.broadcast_to(row, (8, BLOCK)).astype(BF16), spread)
    return wide[:1].astype(I32)


def select_codes(chosen, codes):
    high = dot(chosen, (codes >> 6).astype(F32).astype(BF16))
    low = dot(chosen, (codes & 63).astype(F32).astype(BF16))
    return high.astype(I32) * 64 + low.astype(I32)


def project_kernel(
    place, mask, temporal, w_in, codes, o0, o1, o2, o3, chosen, keeps_o, goes_o, code_o, rows
):
    audio, rank, count = ranks(mask)
    leaves = own_row(jnp.where(audio & (rank >= AUDIO), rank - AUDIO, -1.0), place[4])
    code_o[...] = select_codes(ones_where(leaves.astype(I32) == iota((EXTRA, BLOCK), 0)), codes[...])
    keeps = jnp.where(audio & (rank < AUDIO), rank, -1.0).astype(I32)
    goes = jnp.where(audio & (rank >= AUDIO), rank + AUDIO - count, -1.0).astype(I32)
    keeps_o[...] = keeps
    goes_o[...] = goes
    slots = iota((AUDIO, BLOCK), 0)
    for b in range(TPS):
        o = b ^ 8
        mine = dot(ones_where(keeps[b : b + 1] == slots), temporal[b * BLOCK : (b + 1) * BLOCK, :])
        theirs = dot(ones_where(goes[o : o + 1] == slots), temporal[o * BLOCK : (o + 1) * BLOCK, :])
        chosen[b * AUDIO : (b + 1) * AUDIO, :] = (mine + theirs).astype(BF16)
    for d, out in enumerate((o0, o1, o2, o3)):
        for x in range(4):
            source = pl.ds(pl.multiple_of((x * 4 + (place[3] ^ d)) * AUDIO, AUDIO), AUDIO)
            rows[x * AUDIO : (x + 1) * AUDIO, :] = chosen[source, :]
        out[...] = dot(rows[...], w_in[...]).astype(out.dtype)


def project_meet_kernel(place, p0, p1, p2, p3, o0, o1, o2, o3, total):
    total[...] = p0[...] + p1[...].astype(F32) + p2[...].astype(F32) + p3[...].astype(F32)
    for d, out in enumerate((o0, o1, o2, o3)):
        rows = pl.ds(pl.multiple_of((place[2] ^ d) * AUDIO, AUDIO), AUDIO)
        out[...] = total[rows, :].astype(out.dtype)


def leave_kernel(place, mask, cot, cot_o):
    audio, rank, _ = ranks(mask)
    row = own_row(jnp.where(audio & (rank >= AUDIO), rank - AUDIO, -1.0), place[4])
    wide = each_book(row)
    key = jnp.where(wide >= 0, wide * BOOKS + iota(wide.shape, 1) % BOOKS, -1)
    spread = ones_where(key == iota((EXTRA * BOOKS, BLOCK * BOOKS), 0))
    for i in range(2):
        cols = slice(i * 512, (i + 1) * 512)
        cot_o[:, cols] = dot(spread, cot[:, cols]).astype(BF16)


def embed_kernel(place, mask, codes, codes_come, table, adapter_b, tokens_o, low_o, embedded_o):
    audio, rank, count = ranks(mask)
    row = own_row(jnp.where(audio & (rank < AUDIO), rank, -1.0), place[4]).astype(I32)
    have = own_row(count, place[4]).astype(I32)
    comes = jnp.broadcast_to(have, (1, EXTRA)) + iota((1, EXTRA), 1)
    tokens = select_codes(ones_where(row == iota((AUDIO, BLOCK), 0)), codes[...])
    tokens = tokens + select_codes(ones_where(comes == iota((AUDIO, EXTRA), 0)), codes_come[...])
    tokens_o[...] = tokens
    vocab = iota((AUDIO, VOCAB), 1)
    for k in range(BOOKS):
        rows = slice(k * AUDIO, (k + 1) * AUDIO)
        low = dot(ones_where(tokens[:, k : k + 1] == vocab), table[k]).astype(BF16)
        low_o[rows, :] = low
        embedded_o[rows, :] = dot(low, adapter_b[k])


def upstream_kernel(place, mask, cot, cot_come, w_out, cot_o, weights_o, grad_low_o, grad_mixed_o):
    audio, rank, count = ranks(mask)
    row = own_row(jnp.where(audio & (rank < AUDIO), rank, -1.0), place[4])
    have = own_row(count, place[4])
    slot = iota((ROWS, 128), 0)
    slot = (slot // SPAN) * GROUP + slot % GROUP
    weights = jnp.where(slot < have.astype(I32), AUDIO / have, AUDIO / (BLOCK - have))
    weights_o[...] = weights

    def target(at, book):
        return jnp.where((at >= 0) & (at < AUDIO), (at // GROUP) * SPAN + book * GROUP + at % GROUP, -1)

    wide = each_book(row)
    stays = ones_where(target(wide, iota(wide.shape, 1) % BOOKS) == iota((ROWS, BLOCK * BOOKS), 0))
    index = iota((1, EXTRA * BOOKS), 1)
    come = jnp.broadcast_to(have.astype(I32), index.shape) + index // BOOKS
    comes = ones_where(target(come, index % BOOKS) == iota((ROWS, EXTRA * BOOKS), 0))
    for i in range(2):
        cols = slice(i * 512, (i + 1) * 512)
        here = dot(stays, cot[:, cols]) + dot(comes, cot_come[:, cols])
        cot_o[:, cols] = here.astype(BF16)
        grad_low_o[:, cols] = (here * weights[:, :1]).astype(BF16)
    for i in range(4):
        cols = slice(i * 256, (i + 1) * 256)
        grad_mixed_o[:, cols] = dot(grad_low_o[...], w_out[cols, :], NT).astype(BF16)


def split(a):
    first = iota((SPAN, 128), 1) < 64
    zero = jnp.zeros_like(a)
    return jnp.concatenate([jnp.where(first, a, zero), jnp.where(first, zero, a)], axis=0)


def pick(a):
    return jnp.where(iota((SPAN, 128), 1) < 64, a[:SPAN], a[SPAN:])


def pair_columns(part, p):
    return pl.ds(pl.multiple_of(part * WIDTH + p * 128, 128), 128)


def pair_probs(p, g):
    return pl.ds(pl.multiple_of((p * GROUPS + g) * SPAN, SPAN), SPAN)


SCALE = 1.0 / math.sqrt(64)


def forward_kernel(
    p0, p1, p2, p3, embedded, gain, w_qkv, normed_o, mixed_o, packed_o, stream_o, inv_o, probs_o
):
    for g in range(GROUPS):
        frames = pl.ds(g * GROUP, GROUP)
        proj = p0[frames, :] + p1[frames, :].astype(F32) + p2[frames, :].astype(F32) + p3[frames, :].astype(F32)
        proj = proj.astype(BF16).astype(F32)
        for k in range(BOOKS):
            rows = pl.ds(g * SPAN + k * GROUP, GROUP)
            x = proj + embedded[pl.ds(k * AUDIO + g * GROUP, GROUP), :]
            stream_o[rows, :] = x
            a = lax.rsqrt(jnp.mean(x * x, axis=-1, keepdims=True) + 1e-05)
            inv_o[rows, :] = jnp.broadcast_to(a, (GROUP, 128))
            normed_o[rows, :] = (x * a * gain[...]).astype(BF16)

    tile = 512

    @pl.loop(0, 3 * WIDTH // tile)
    def _(i):
        cols = pl.ds(pl.multiple_of(i * tile, tile), tile)
        packed_o[:, cols] = dot(normed_o[...], w_qkv[:, cols]).astype(BF16)

    key_row = iota((SPAN, 2 * SPAN), 0)
    query_row = iota((SPAN, 2 * SPAN), 1) % SPAN
    allowed = (key_row % GROUP == query_row % GROUP) & (key_row // GROUP <= query_row // GROUP)

    @pl.loop(0, HEADS // 8)
    def _(half):
        for p, g in ((half * 4 + i, g) for i in range(4) for g in range(GROUPS)):
            rows = pl.ds(g * SPAN, SPAN)
            query = split(packed_o[rows, pair_columns(0, p)])
            keys = packed_o[rows, pair_columns(1, p)]
            values = packed_o[rows, pair_columns(2, p)]
            scores = jnp.where(allowed, dot(keys, query, NT) * SCALE, -1e30)
            top = jnp.max(scores, axis=0, keepdims=True)
            e = jnp.exp(scores - top)
            probs = e * (1.0 / jnp.sum(e, axis=0, keepdims=True))
            probs_o[pair_probs(p, g), :] = probs
            mixed = pick(dot(probs.astype(BF16), values, TN))
            mixed_o[rows, pair_columns(0, p)] = mixed.astype(BF16)


def backward_kernel(packed, probs_in, grad_mixed, packed_grad_o):
    @pl.loop(0, HEADS // 8)
    def _(half):
        for p, g in ((half * 4 + i, g) for i in range(4) for g in range(GROUPS)):
            rows = pl.ds(g * SPAN, SPAN)
            query = split(packed[rows, pair_columns(0, p)])
            keys = packed[rows, pair_columns(1, p)]
            values = packed[rows, pair_columns(2, p)]
            gm = split(grad_mixed[rows, pair_columns(0, p)])
            probs = probs_in[pair_probs(p, g), :]
            grad_probs = dot(values, gm, NT)
            packed_grad_o[rows, pair_columns(2, p)] = dot(probs.astype(BF16), gm).astype(BF16)
            inner = jnp.sum(probs * grad_probs, axis=0, keepdims=True)
            grad_scores = (probs * (grad_probs - inner) * SCALE).astype(BF16)
            grad_query = pick(dot(grad_scores, keys, TN))
            packed_grad_o[rows, pair_columns(0, p)] = grad_query.astype(BF16)
            packed_grad_o[rows, pair_columns(1, p)] = dot(grad_scores, query).astype(BF16)


def norm_kernel(
    packed_grad, w_qkv, stream, inv, cot, weights, gain, adapter_b,
    tokens, message_o, stream_low_o, gain_o, grad_normed,
):
    tile = 256

    @pl.loop(0, WIDTH // tile)
    def _(i):
        cols = pl.ds(pl.multiple_of(i * tile, tile), tile)
        grad_normed[:, cols] = dot(packed_grad[...], w_qkv[cols, :], NT)

    gain_sum = jnp.zeros((GROUP, WIDTH), F32)
    for g in range(GROUPS):
        total = jnp.zeros((GROUP, WIDTH), F32)
        for k in range(BOOKS):
            rows = pl.ds(g * SPAN + k * GROUP, GROUP)
            x = stream[rows, :]
            a = inv[rows, :][:, :1]
            gn = grad_normed[rows, :]
            gain_sum = gain_sum + gn * (x * a)
            scaled = gn * gain[...]
            mean = jnp.mean(scaled * x, axis=-1, keepdims=True)
            grad_out = cot[rows, :].astype(F32) * weights[rows, :][:, :1]
            gs = grad_out + a * (scaled - x * (a * a * mean))
            total = total + gs
            stream_low_o[pl.ds(k * AUDIO + g * GROUP, GROUP), :] = gs.astype(BF16)
        message_o[pl.ds(g * GROUP, GROUP), :WIDTH] = total.astype(BF16)
    gain_row = jnp.sum(gain_sum, axis=0, keepdims=True)
    for i in range(WIDTH // 128):
        piece = jnp.broadcast_to(gain_row[:, i * 128 : (i + 1) * 128], (128, 128))
        gain_o[i * 128 : (i + 1) * 128, :] = jnp.transpose(piece)
    for k in range(BOOKS):
        rows = pl.ds(k * AUDIO, AUDIO)
        lowrank = dot(stream_low_o[rows, :], adapter_b[k], NT).astype(BF16)
        message_o[AUDIO:, k * RANK : (k + 1) * RANK] = lowrank
    marks = jnp.zeros((AUDIO, RANK), F32)
    for k in range(BOOKS):
        token = jnp.broadcast_to(tokens[:, k : k + 1], (AUDIO, RANK))
        lane = iota((AUDIO, RANK), 1)
        marks = jnp.where(lane == k, (token >> 6).astype(F32), marks)
        marks = jnp.where(lane == BOOKS + k, (token & 63).astype(F32), marks)
    message_o[:AUDIO, WIDTH:] = marks.astype(BF16)
    message_o[AUDIO:, WIDTH:] = jnp.zeros((AUDIO, RANK), BF16)


def columns_of(a, core, order):
    return [jnp.transpose(a[:, pl.ds(pl.multiple_of((z * 2 + core) * 128, 128), 128)]) for z in order]


def give_kernel(place, normed, packed_grad, out, lhs):
    for i, block in enumerate(columns_of(normed, 1 - place[1], range(4))):
        lhs[i * 128 : (i + 1) * 128, :] = block
    tile = 512
    for i in range(LEFT // tile):
        cols = slice(i * tile, (i + 1) * tile)
        r = dot(lhs[...], packed_grad[:, cols]).astype(BF16)
        for z in range(4):
            out[z, :, cols] = r[z * 128 : (z + 1) * 128]


def backward_give_kernel(place, packed, probs_in, grad_mixed, normed, packed_grad_o, give_o, lhs):
    backward_kernel(packed, probs_in, grad_mixed, packed_grad_o)
    give_kernel(place, normed, packed_grad_o, give_o, lhs)


def norm_give_kernel(
    place, packed_grad, w_qkv, stream, inv, cot, weights, gain, adapter_b, tokens, mixed, grad_low, low,
    message_o, stream_low_o, gain_o, give_o, grad_normed, lhs,
):
    norm_kernel(
        packed_grad, w_qkv, stream, inv, cot, weights, gain, adapter_b, tokens,
        message_o, stream_low_o, gain_o, grad_normed,
    )
    give_late_kernel(place, mixed, grad_low, low, stream_low_o, gain_o, give_o, lhs)


def keep_left_kernel(place, normed, packed_grad, got, l0, l1, l2, l3, lhs):
    outs = (l0, l1, l2, l3)
    order = [place[0] ^ d for d in range(4)]
    for i, block in enumerate(columns_of(normed, place[1], order)):
        lhs[i * 128 : (i + 1) * 128, :] = block
    tile = 512
    for i in range(LEFT // tile):
        cols = slice(i * tile, (i + 1) * tile)
        r = dot(lhs[...], packed_grad[:, cols])
        for d in range(4):
            total = r[d * 128 : (d + 1) * 128] + got[order[d], :, cols].astype(F32)
            outs[d][:, cols] = total.astype(outs[d].dtype)


def rank_rows(low, rank, book):
    chosen = dot(ones_where(rank == iota((512, RANK), 1)), low[...], NT)
    return jnp.where(iota((512, ROWS), 1) // AUDIO == book, chosen, 0.0).astype(BF16)


def give_late_kernel(place, mixed, grad_low, low, stream_low, gain_col, out, lhs):
    other = 1 - place[1]
    for i, block in enumerate(columns_of(mixed, other, range(4))):
        lhs[i * 128 : (i + 1) * 128, :] = block
    row = iota((512, 1), 0)
    lhs2 = rank_rows(low, (row // 128) * 32 + other * 16 + (row % 128) // 8, row % 8)
    tile = 512
    for j, (left, right) in enumerate(((lhs[...], grad_low), (lhs2, stream_low))):
        for i in range(WIDTH // tile):
            r = dot(left, right[:, i * tile : (i + 1) * tile]).astype(BF16)
            at = j * WIDTH + i * tile
            for z in range(4):
                out[z, :, at : at + tile] = r[z * 128 : (z + 1) * 128]
    for z in range(4):
        rows = pl.ds(pl.multiple_of((z * 2 + other) * 128, 128), 128)
        out[z, :, 2 * WIDTH :] = gain_col[rows, :].astype(BF16)


def keep_right_kernel(place, mixed, grad_low, low, stream_low, gain_col, got, r0, r1, r2, r3, lhs, square):
    outs = (r0, r1, r2, r3)
    core = place[1]
    for z, block in enumerate(columns_of(mixed, core, range(4))):
        lhs[z * 128 : (z + 1) * 128, :] = block
    row = iota((512, 1), 0)
    lhs2 = rank_rows(low, (row // 128) * 32 + core * 16 + (row % 128) // 8, row % 8)

    def give(z, total, cols):
        square[...] = total
        for d, out in enumerate(outs):
            rows = pl.ds(pl.multiple_of((place[2] ^ d) * 32, 32), 32)
            out[z, :, cols] = square[rows, :].astype(out.dtype)

    tile = 512
    for j, (left, right) in enumerate(((lhs[...], grad_low), (lhs2, stream_low))):
        for i in range(WIDTH // tile):
            r = dot(left, right[:, i * tile : (i + 1) * tile])
            cols = slice(j * WIDTH + i * tile, j * WIDTH + (i + 1) * tile)
            for z in range(4):
                give(z, r[z * 128 : (z + 1) * 128] + got[z, :, cols].astype(F32), cols)
    cols = slice(2 * WIDTH, RIGHT)
    for z in range(4):
        rows = pl.ds(pl.multiple_of((z * 2 + core) * 128, 128), 128)
        total = gain_col[rows, :] + got[z, :, cols].astype(F32)
        for d, out in enumerate(outs):
            square[:, :GAIN] = total
            part = square[pl.ds(pl.multiple_of((place[2] ^ d) * 32, 32), 32), :]
            out[z, :, cols] = part[:, :GAIN].astype(out.dtype)


def table_kernel(place, m0, m1, m2, m3, give_o, keep_o, square):
    core = place[1]
    for k in range(BOOKS):
        lanes = slice(k * RANK, (k + 1) * RANK)
        lowrank = jnp.concatenate([m[AUDIO:, lanes] for m in (m0, m1, m2, m3)], axis=0)
        marks = jnp.concatenate([m[:AUDIO, WIDTH:] for m in (m0, m1, m2, m3)], axis=0).astype(F32)
        high = marks[:, k : k + 1].astype(I32)
        low = marks[:, BOOKS + k : BOOKS + k + 1].astype(I32)
        at = jnp.where(high % 4 == place[2], (high // 4) * 64 + low, -1)
        spread = ones_where(at == iota((4 * AUDIO, 512), 1))
        square[k * 512 : (k + 1) * 512, :] = dot(spread, lowrank, TN)
    for half, out in ((1 - core, give_o), (core, keep_o)):
        for z in range(4):
            for r in range(16):
                at = (z * 2 + half) * 64 + r
                block = [square[pl.ds(at + y * 16, 8, stride=512), :] for y in range(4)]
                out[z, :, r * 128 : (r + 1) * 128] = jnp.concatenate(block, axis=0).astype(out.dtype)


def win_kernel(place, p0, p1, p2, p3, chosen, give_o, keep_o, order, rows):
    core = place[1]
    for dy, p in enumerate((p0, p1, p2, p3)):
        for dx in range(4):
            device = (place[2] ^ dx) * 4 + (place[3] ^ dy)
            here = (dy * 4 + dx) * AUDIO
            source = pl.ds(pl.multiple_of(device * AUDIO, AUDIO), AUDIO)
            order[here : here + AUDIO, :] = chosen[source, :]
            rows[here : here + AUDIO, :] = p[dx * AUDIO : (dx + 1) * AUDIO, :]
    features = jnp.transpose(order[...])
    for half, out in ((1 - core, give_o), (core, keep_o)):
        for z in range(4):
            cols = pl.ds(pl.multiple_of((z * 2 + half) * 128, 128), 128)
            out[z] = dot(features, rows[:, cols]).astype(out.dtype)


def win_meet_kernel(place, keep, got, o0, o1, o2, o3):
    for d, out in enumerate((o0, o1, o2, o3)):
        z = place[0] ^ d
        out[...] = (keep[z] + got[z].astype(F32)).astype(out.dtype)


def left_kernel(place, l0, g1, g2, g3, o0, o1, o2, o3, total):
    total[...] = l0[...] + g1[...].astype(F32) + g2[...].astype(F32) + g3[...].astype(F32)
    for d, out in enumerate((o0, o1, o2, o3)):
        rows = pl.ds(pl.multiple_of((place[2] ^ d) * 32, 32), 32)
        out[...] = total[rows, :].astype(out.dtype)


def right_kernel(place, r0, g1, g2, g3, keep, got, o0, o1, o2, o3):
    for d, out in enumerate((o0, o1, o2, o3)):
        z = place[0] ^ d
        total = r0[z] + g1[z].astype(F32) + g2[z].astype(F32) + g3[z].astype(F32)
        out[:, :RIGHT] = total.astype(out.dtype)
        out[:, RIGHT:] = (keep[z] + got[z].astype(F32)).astype(out.dtype)


def meet_kernel(place, l0, l1, l2, l3, r0, r1, r2, r3, o0, o1, o2, o3, left, right):
    left[...] = l0[...] + l1[...].astype(F32) + l2[...].astype(F32) + l3[...].astype(F32)
    right[...] = r0[...] + r1[...].astype(F32) + r2[...].astype(F32) + r3[...].astype(F32)
    half = LEFT // 2
    for d, out in enumerate((o0, o1, o2, o3)):
        rows = pl.ds(pl.multiple_of((place[3] ^ d) * 8, 8), 8)
        out[:, :half] = jnp.concatenate([left[rows, :half], left[rows, half:]], axis=0).astype(out.dtype)
        block = right[rows, RIGHT:]
        block = jnp.concatenate([block, jnp.zeros((8, RIGHT - TABLE), F32)], axis=1)
        out[:, half:] = jnp.concatenate([right[rows, :RIGHT], block], axis=0).astype(out.dtype)


def last_kernel(a, b, c, d, qkv_o, wout_o, b_o, gain_o, table_o):
    total = a[...] + b[...].astype(F32) + c[...].astype(F32) + d[...].astype(F32)
    half = LEFT // 2
    qkv_o[:, :half] = total[:8, :half]
    qkv_o[:, half:] = total[8:, :half]
    wout_o[...] = total[:8, half : half + WIDTH]
    b_o[:, 0, :] = total[:8, half + WIDTH : half + 2 * WIDTH]
    gain_o[...] = total[:8, half + 2 * WIDTH :]
    for r in range(16):
        table_o[:, r, :] = total[8:, half + r * 128 : half + (r + 1) * 128]


def temporal_kernel(place, keeps, goes, p0, p1, p2, p3, w_in, out, grad):
    for dy, p in enumerate((p0, p1, p2, p3)):
        grad[dy * 192 : (dy + 1) * 192, :] = dot(p[...], w_in[...], NT).astype(BF16)
    slots = iota((AUDIO, BLOCK), 0)

    def of_device(x, y):
        at = ((y ^ place[3]) * 4 + (x ^ place[2])) * AUDIO
        return grad[pl.ds(pl.multiple_of(at, AUDIO), AUDIO), :]

    for b in range(TPS):
        x, y = b // 4, b % 4
        mine = dot(ones_where(keeps[b : b + 1] == slots), of_device(x, y), TN)
        theirs = dot(ones_where(goes[b : b + 1] == slots), of_device(x ^ 2, y), TN)
        out[b * BLOCK : (b + 1) * BLOCK, :] = (mine + theirs).astype(BF16)


def swap(x, axis, n, d):
    return lax.ppermute(x, axis, [(i, i ^ d) for i in range(n)])


def swaps(parts, axis):
    return (parts[0],) + tuple(swap(parts[d], axis, 4, d) for d in (1, 2, 3))


def after(x, *others):
    return lax.optimization_barrier((x,) + others)[0]


def to_all(x, axes):
    return lax.all_to_all(x, axes, 0, 0, tiled=True)


def local(
    temporal, w_in, audio_mask, counts, codes, cotangent, norm_gain, w_qkv, w_out, adapter_a, adapter_b
):
    x_at, y_at = lax.axis_index("x"), lax.axis_index("y")
    z_at, c_at = lax.axis_index("z"), lax.axis_index("c")
    place = jnp.stack([z_at, c_at, x_at, y_at, x_at * 4 + y_at]).astype(I32)
    mask = audio_mask.reshape(TPS, BLOCK)
    cot_rows = cotangent.reshape(BLOCK * BOOKS, WIDTH)
    gain = norm_gain.reshape(1, WIDTH)

    group = 4 * AUDIO
    *parts, chosen, keeps, goes, code_leave = call(
        project_kernel, "project",
        (shaped(group, WIDTH, dtype=F32),) + (shaped(group, WIDTH),) * 3
        + (shaped(TPS * AUDIO, 256), shaped(TPS, BLOCK, dtype=I32), shaped(TPS, BLOCK, dtype=I32),
           shaped(EXTRA, BOOKS, dtype=I32)),
        (place, mask, temporal, w_in, codes), scalars=1, scratch=[pltpu.VMEM((group, 256), BF16)],
    )
    code_come = swap(code_leave, "x", 4, 2)
    near = [swap(parts[d], "y", 4, d) for d in (1, 3)]
    cot_leave = call(
        leave_kernel, "leave", shaped(EXTRA * BOOKS, WIDTH), (after(place, chosen), mask, cot_rows), scalars=1,
    )
    far, cot_leave, code_come, *near = lax.optimization_barrier((parts[2], cot_leave, code_come, *near))
    parts = (parts[0], near[0], swap(far, "y", 4, 2), near[1])
    cot_come = swap(cot_leave, "x", 4, 2)
    tokens, low, embedded = call(
        embed_kernel, "embed",
        (shaped(AUDIO, BOOKS, dtype=I32), shaped(ROWS, RANK), shaped(ROWS, WIDTH, dtype=F32)),
        (after(place, code_come), mask, codes, code_come, adapter_a, adapter_b), scalars=1,
    )
    parts = call(
        project_meet_kernel, "project_meet", (shaped(AUDIO, WIDTH, dtype=F32),) + (shaped(AUDIO, WIDTH),) * 3,
        (after(place, low),) + parts, scalars=1, scratch=[pltpu.VMEM((group, WIDTH), F32)],
    )
    parts = swaps(parts, "x")
    cot, weights, grad_low, grad_mixed = call(
        upstream_kernel, "upstream",
        (shaped(ROWS, WIDTH), shaped(ROWS, 128, dtype=F32), shaped(ROWS, WIDTH), shaped(ROWS, WIDTH)),
        (after(place, parts[0]), mask, cot_rows, cot_come, w_out), scalars=1,
    )
    normed, mixed, packed, stream, inv, probs = call(
        forward_kernel, "forward",
        (shaped(ROWS, WIDTH), shaped(ROWS, WIDTH), shaped(ROWS, 3 * WIDTH),
         shaped(ROWS, WIDTH, dtype=F32), shaped(ROWS, 128, dtype=F32),
         shaped(HEADS // 2 * ROWS, 256, dtype=F32)),
        (*parts, embedded, after(gain, grad_mixed), w_qkv), limit=16,
    )
    grad_packed, give = call(
        backward_give_kernel, "backward", (shaped(ROWS, 3 * WIDTH), shaped(4, 128, LEFT)),
        (place, packed, probs, grad_mixed, normed), scalars=1,
        scratch=[pltpu.VMEM((512, ROWS), BF16)], limit=12,
    )
    got_left = swap(give, "c", 2, 1)
    message, stream_low, gain_col, give_late = call(
        norm_give_kernel, "norm",
        (shaped(2 * AUDIO, WIDTH + RANK), shaped(ROWS, WIDTH), shaped(WIDTH, 128, dtype=F32), shaped(4, 128, RIGHT)),
        (place, grad_packed, w_qkv, stream, inv, cot, weights, gain, adapter_b, tokens, mixed, grad_low, low),
        scalars=1, scratch=[pltpu.VMEM((ROWS, WIDTH), F32), pltpu.VMEM((512, ROWS), BF16)], limit=16,
    )
    got_late = swap(give_late, "c", 2, 1)
    messages = swaps((message,) * 4, "x")
    lefts = call(
        keep_left_kernel, "keep_left",
        (shaped(128, LEFT, dtype=F32),) + (shaped(128, LEFT),) * 3,
        (after(place, message), normed, grad_packed, got_left), scalars=1,
        scratch=[pltpu.VMEM((512, ROWS), BF16)],
    )
    rights = call(
        keep_right_kernel, "keep_right",
        (shaped(4, 32, RIGHT, dtype=F32),) + (shaped(4, 32, RIGHT),) * 3,
        (after(place, lefts[1]), mixed, grad_low, low, stream_low, gain_col, got_late),
        scalars=1, scratch=[pltpu.VMEM((512, ROWS), BF16), pltpu.VMEM((128, 512), F32)],
    )
    give_table, keep_table = call(
        table_kernel, "table",
        (shaped(4, 32, TABLE), shaped(4, 32, TABLE, dtype=F32)),
        (after(place, rights[1]),) + messages, scalars=1, scratch=[pltpu.VMEM((BOOKS * 512, 128), F32)],
    )
    got_table = swap(give_table, "c", 2, 1)
    near = [swap(lefts[d], "z", 4, d) for d in (1, 3)] + [swap(rights[d], "x", 4, d) for d in (1, 3)]
    piece = jnp.concatenate([m[:AUDIO, :WIDTH] for m in messages], axis=0)
    far_left, far_right, piece, got_table, *near = lax.optimization_barrier(
        (lefts[2], rights[2], piece, got_table, *near)
    )
    far_left, far_right = swap(far_left, "z", 4, 2), swap(far_right, "x", 4, 2)
    lefts = (lefts[0], near[0], far_left, near[1])
    rights = (rights[0], near[2], far_right, near[3])
    pieces = swaps((piece,) * 4, "y")
    rights = call(
        right_kernel, "right", (shaped(32, RIGHT + TABLE, dtype=F32),) + (shaped(32, RIGHT + TABLE),) * 3,
        (place,) + rights + (keep_table, got_table), scalars=1,
    )
    rights = swaps(rights, "z")
    lefts = call(
        left_kernel, "left", (shaped(32, LEFT, dtype=F32),) + (shaped(32, LEFT),) * 3,
        (place,) + lefts, scalars=1, scratch=[pltpu.VMEM((128, LEFT), F32)],
    )
    lefts = swaps(lefts, "x")
    give_win, keep_win = call(
        win_kernel, "win", (shaped(4, 256, 128), shaped(4, 256, 128, dtype=F32)),
        (place,) + pieces + (chosen,), scalars=1,
        scratch=[pltpu.VMEM((TPS * AUDIO, 256), BF16), pltpu.VMEM((TPS * AUDIO, WIDTH), BF16)],
    )
    got_win = swap(give_win, "c", 2, 1)
    wins = call(
        win_meet_kernel, "win_meet", (shaped(256, 128, dtype=F32),) + (shaped(256, 128),) * 3,
        (place, keep_win, got_win), scalars=1,
    )
    wins = swaps(wins, "z")
    columns = LEFT // 2 + RIGHT
    meets = call(
        meet_kernel, "meet", (shaped(16, columns, dtype=F32),) + (shaped(16, columns),) * 3,
        (place,) + lefts + rights, scalars=1,
        scratch=[pltpu.VMEM((32, LEFT), F32), pltpu.VMEM((32, RIGHT + TABLE), F32)],
    )
    grad_temporal = call(
        temporal_kernel, "temporal", shaped(TPS * BLOCK, 256),
        (after(place, meets[1]), keeps, goes) + pieces + (w_in,), scalars=1,
        scratch=[pltpu.VMEM((TPS * AUDIO, 256), BF16)],
    )
    meets = swaps(meets, "y")
    grad_win = wins[0] + wins[1].astype(F32) + wins[2].astype(F32) + wins[3].astype(F32)
    grad_wqkv, grad_wout, grad_b, grad_gain, grad_a = call(
        last_kernel, "last",
        (shaped(8, LEFT, dtype=F32), shaped(8, WIDTH, dtype=F32), shaped(BOOKS, 1, WIDTH, dtype=F32),
         shaped(8, GAIN, dtype=F32), shaped(BOOKS, 16, RANK, dtype=F32)),
        meets,
    )
    return (
        grad_temporal,
        grad_win,
        grad_gain[:, 0],
        grad_wqkv,
        grad_wout,
        grad_a,
        grad_b,
    )


def solution(mesh):
    grid = Mesh(mesh.devices.reshape(4, 2, 4, 4), ("z", "c", "x", "y"))
    seq, tp = ("z", "c"), ("x", "y")
    every = seq + tp
    placed = (
        P(seq, tp),
        P(tp, None),
        P(seq),
        P(),
        P(every, None),
        P(every, None, None),
        P(),
        P(),
        P(),
        P(),
        P(),
    )
    return jax.shard_map(
        local,
        mesh=grid,
        in_specs=placed,
        out_specs=(
            P(seq, tp),
            P(tp, seq),
            P(every),
            P(every, None),
            P(every, None),
            P(None, every, None),
            P(None, every, None),
        ),
        check_vma=False,
    )
```

time: 2470 us -> 154 us (0.06)
  waiting for transfers between devices: 2150 us -> 46.1 us
  matrix products: 87.3 us -> 0 us
  local copies, waits for them, and re-layouts: 85.3 us -> 9.84 us
  blocking collectives: 65 us -> 0 us
  Pallas kernels: 0 us -> 48.4 us
  starting transfers between devices: 0.29 us -> 47.9 us
  other arithmetic: 37.4 us -> 0.71 us
    reduce_scatter x6 -> x0, waiting for transfers between devices: 2110 us -> none  [the longest x1 647 us: local(): lax.psum_scatter(grad_a, ('seq', 'tp'), scatter_dimension=1, tiled=True)]
    dot_general x18 -> x0, matrix products: 87.3 us -> none  [the longest x1 12.6 us: attention_backward(): jnp.einsum('nf,df->nd', grad_packed, w_qkv, preferred_element_type=jnp.fl...]
    unnamed x1 -> x0, blocking collectives: 65 us -> none
    pallas_call x0 -> x18, Pallas kernels: none -> 48.4 us  [call(): pl.pallas_call(kernel, out_shape=out, in_specs=[smem] * scalars + [vmem]...]
    ppermute x0 -> x36, starting transfers between devices: none -> 47.9 us  [swap(): return lax.ppermute(x, axis, [(i, i ^ d) for i in range(n)])]
    all_gather x1 -> x0, waiting for transfers between devices: 46.8 us -> none  [local(): piece = lax.all_gather(grad_block, 'tp', axis=0, tiled=True)]
    ppermute x0 -> x36, waiting for transfers between devices: none -> 46.1 us  [swap(): return lax.ppermute(x, axis, [(i, i ^ d) for i in range(n)])]
    reshape x5 -> x1, local copies, waits for them, and re-layouts: 33.1 us -> 0.91 us  [local(): mask = audio_mask.reshape(TPS, BLOCK)]
  transfers between devices with their start and end apart: 7 -> 36, of which waited for: 6 -> 15; matrix products, arithmetic and copies ran while one was open for 4% -> 0% of each run, Pallas kernels for 0% -> 20%
where the time goes in v1:
time: 154 us
  Pallas kernels  48.4 us (31%)
  starting transfers between devices  47.9 us (31%)
  waiting for transfers between devices  46.1 us (30%)
  local copies, waits for them, and re-layouts  9.84 us (6%)
    pallas_call x18, Pallas kernels, call(): pl.pallas_call(kernel, out_shape=out, in_specs=[smem] * scalars + [vmem]...  48.4 us
    ppermute x36, starting transfers between devices, swap(): return lax.ppermute(x, axis, [(i, i ^ d) for i in range(n)])  47.9 us
    ppermute x36, waiting for transfers between devices, swap(): return lax.ppermute(x, axis, [(i, i ^ d) for i in range(n)])  46.1 us
    unnamed x23, local copies, waits for them, and re-layouts  8.18 us
  transfers between devices with their start and end apart: 36, of which 15 were waited for; matrix products, arithmetic and copies ran while one was open for 0% of the time, Pallas kernels for 20%

profile of v1, /device:TPU:2, one launch (start us, length us, event | category | flops | bytes accessed | tf_op | source)
XLA Modules:
  0.0 153.9 jit_solution(16498958338316459381)
XLA Ops:
  4.6 1.6 %project.1 = (f32[192,1024]{1,0:T(8,128)S(1)}, bf16[192,1024]{1,0:T(8,128)(2,1)S(1)}, bf16[192,1024]{1,0:T(8,128)(2,1)S(1)}, bf16[192,1024]{1,0:T(8,128)(2,1)S(1...) custom-call(s32[5]{0:T(128)S(1)} %stack.23.place, ...), custom_call_target="tpu_custom_call" | custom-call | tf_op jit(solution)/shard_map/project/pallas_call | solution.py:56
  6.2 1.7 %collective-permute-start.1 = (bf16[192,1024]{1,0:T(8,128)(2,1)S(1)}, bf16[192,1024]{1,0:T(8,128)(2,1)S(1)}, u32[]{:S(2)}, u32[]{:S(2)}) collective-permute-start(bf16[192,1024]{1,0:T(8,128)(2,1)S(1)} %get-tuple-element.97), channel_id=1, source_target_pairs={{0,1},{1,0},{2,3},{3,2},{4,5},{5,4},{6,7},{7,6},{8,9},{9,8},{10,11... | collective-permute-start | bytes 1179656 | tf_op jit(solution)/shard_map/ppermute | solution.py:499
  7.9 2.2 %collective-permute-start.2 = (bf16[192,1024]{1,0:T(8,128)(2,1)S(1)}, bf16[192,1024]{1,0:T(8,128)(2,1)S(1)}, u32[]{:S(2)}, u32[]{:S(2)}) collective-permute-start(bf16[192,1024]{1,0:T(8,128)(2,1)S(1)} %get-tuple-element.98), channel_id=1, source_target_pairs={{0,3},{1,2},{2,1},{3,0},{4,7},{5,6},{6,5},{7,4},{8,11},{9,10},{10,... | collective-permute-start | bytes 1179656 | tf_op jit(solution)/shard_map/ppermute | solution.py:499
  10.1 2.1 %collective-permute-start = (s32[40,8]{1,0:T(8,128)S(1)}, s32[40,8]{1,0:T(8,128)S(1)}, u32[]{:S(2)}, u32[]{:S(2)}) collective-permute-start(s32[40,8]{1,0:T(8,128)S(1)} %get-tuple-element.96), channel_id=1, source_target_pairs={{0,8},{4,12},{8,0},{12,4},{1,9},{5,13},{9,1},{13,5},{2,10},{6,14},... | collective-permute-start | bytes 3848 | tf_op jit(solution)/shard_map/ppermute | solution.py:499
  12.2 1.4 copy-done.1
  13.6 1.5 leave.1
  15.3 1.8 %collective-permute-done.1.p1 = bf16[192,1024]{1,0:T(8,128)(2,1)S(1)} collective-permute-done((bf16[192,1024]{1,0:T(8,128)(2,1)S(1)}, bf16[192,1024]{1,0:T(8,128)(2,1)S(1)}, u32[]{:S(2)}, u32[]{:S(2)}) %collective-permute-start.1) | collective-permute-done | bytes 393248 | tf_op jit(solution)/shard_map/ppermute | solution.py:499
  17.2 2.5 %collective-permute-done.2.p3 = bf16[192,1024]{1,0:T(8,128)(2,1)S(1)} collective-permute-done((bf16[192,1024]{1,0:T(8,128)(2,1)S(1)}, bf16[192,1024]{1,0:T(8,128)(2,1)S(1)}, u32[]{:S(2)}, u32[]{:S(2)}) %collective-permute-start.2) | collective-permute-done | bytes 393248 | tf_op jit(solution)/shard_map/ppermute | solution.py:499
  19.7 2.1 %collective-permute-start.7 = (bf16[320,1024]{1,0:T(8,128)(2,1)S(1)}, bf16[320,1024]{1,0:T(8,128)(2,1)S(1)}, u32[]{:S(2)}, u32[]{:S(2)}) collective-permute-start(bf16[320,1024]{1,0:T(8,128)(2,1)S(1)} %leave.1), channel_id=1, source_target_pairs={{0,8},{4,12},{8,0},{12,4},{1,9},{5,13},{9,1},{13,5},{2,10},{6,14},... | collective-permute-start | bytes 1966088 | tf_op jit(solution)/shard_map/ppermute | solution.py:499
  21.8 1.7 %collective-permute-start.3 = (bf16[192,1024]{1,0:T(8,128)(2,1)S(1)}, bf16[192,1024]{1,0:T(8,128)(2,1)S(1)}, u32[]{:S(2)}, u32[]{:S(2)}) collective-permute-start(bf16[192,1024]{1,0:T(8,128)(2,1)S(1)} %get-tuple-element.105), channel_id=1, source_target_pairs={{0,2},{1,3},{2,0},{3,1},{4,6},{5,7},{6,4},{7,5},{8,10},{9,11},{10,... | collective-permute-start | bytes 1179656 | tf_op jit(solution)/shard_map/ppermute | solution.py:499
  23.5 2.2 %copy-done.3 = bf16[8,2048,128]{2,1,0:T(8,128)(2,1)S(1)} copy-done((bf16[8,2048,128]{2,1,0:T(8,128)(2,1)S(1)}, bf16[8,2048,128]{2,1,0:T(8,128)(2,1)}, u32[]{:S(2)}) %copy-start.3) | copy-done | bytes 4194328
  25.7 2.8 %embed.1 = (s32[48,8]{1,0:T(8,128)S(1)}, bf16[384,128]{1,0:T(8,128)(2,1)S(1)}, f32[384,1024]{1,0:T(8,128)S(1)}) custom-call(s32[5]{0:T(128)S(1)} %stack.23.place, s32[16,96]{1,0:T(8,128)S(1)} %reshape.23.mask, s32[96,8]{1,0:T(8,128)S(1)} %copy.19.codes, s32[40,8]{1,0:T(8,128)S(1)} %collective-permute-done.codes_come, bf16[8,2048,128]{2,1,0:T(8,128)(2,1)S(1)} %copy-done.3, ...), custom_call_target="tpu_custom_call" | custom-call | tf_op jit(solution)/shard_map/embed/pallas_call | solution.py:56
  28.5 4.2 %collective-permute-done.3.p2 = bf16[192,1024]{1,0:T(8,128)(2,1)S(1)} collective-permute-done((bf16[192,1024]{1,0:T(8,128)(2,1)S(1)}, bf16[192,1024]{1,0:T(8,128)(2,1)S(1)}, u32[]{:S(2)}, u32[]{:S(2)}) %collective-permute-start.3) | collective-permute-done | bytes 393248 | tf_op jit(solution)/shard_map/ppermute | solution.py:499
  33.6 1.5 collective-permute-start.4
  35.1 2.0 %collective-permute-start.6 = (bf16[48,1024]{1,0:T(8,128)(2,1)S(1)}, bf16[48,1024]{1,0:T(8,128)(2,1)S(1)}, u32[]{:S(2)}, u32[]{:S(2)}) collective-permute-start(bf16[48,1024]{1,0:T(8,128)(2,1)S(1)} %get-tuple-element.110), channel_id=1, source_target_pairs={{0,12},{4,8},{8,4},{12,0},{1,13},{5,9},{9,5},{13,1},{2,14},{6,10},... | collective-permute-start | bytes 294920 | tf_op jit(solution)/shard_map/ppermute | solution.py:499
  37.1 1.5 collective-permute-done.7.cot_come
  38.7 1.6 %copy-done.6 = bf16[1024,1024]{1,0:T(8,128)(2,1)S(1)} copy-done((bf16[1024,1024]{1,0:T(8,128)(2,1)S(1)}, bf16[1024,1024]{1,0:T(8,128)(2,1)}, u32[]{:S(2)}) %copy-start.6) | copy-done | bytes 2097176
  40.2 2.7 %upstream.1 = (bf16[384,1024]{1,0:T(8,128)(2,1)S(1)}, f32[384,128]{1,0:T(8,128)S(1)}, bf16[384,1024]{1,0:T(8,128)(2,1)S(1)}, bf16[384,1024]{1,0:T(8,128)(2,1)S(1)}) custom-call(s32[5]{0:T(128)S(1)} %stack.23.place, s32[16,96]{1,0:T(8,128)S(1)} %reshape.23.mask, bf16[768,1024]{1,0:T(8,128)(2,1)S(1)} %bitcast.10, ...), custom_call_target="tpu_custom_call" | custom-call | tf_op jit(solution)/shard_map/upstream/pallas_call | solution.py:56
  43.0 6.4 %forward.1 = (bf16[384,1024]{1,0:T(8,128)(2,1)S(1)}, bf16[384,1024]{1,0:T(8,128)(2,1)S(1)}, bf16[384,3072]{1,0:T(8,128)(2,1)S(1)}, f32[384,1024]{1,0:T(8,128)S(1...) custom-call(f32[48,1024]{1,0:T(8,128)S(1)} %get-tuple-element.107.p0, ...), custom_call_target="tpu_custom_call" | custom-call | tf_op jit(solution)/shard_map/forward/pallas_call | solution.py:56
  49.4 8.7 %backward.1 = (bf16[384,3072]{1,0:T(8,128)(2,1)S(1)}, bf16[4,128,3072]{2,1,0:T(8,128)(2,1)S(1)}) custom-call(s32[5]{0:T(128)S(1)} %stack.23.place, bf16[384,3072]{1,0:T(8,128)(2,1)S(1)} %get-tuple-element.116.packed, f32[3072,256]{1,0:T(8,128)S(1)} %get-tuple-element.117.probs_in, bf16[384,1024]{1,0:T(8,128)(2,1)S(1)} %get-tuple-element.114.grad_mixed, ...), custom_call_target="tpu_custom_call" | custom-call | tf_op jit(solution)/shard_map/backward/pallas_call | solution.py:56
  58.2 6.6 %norm.1 = (bf16[96,1152]{1,0:T(8,128)(2,1)S(1)}, bf16[384,1024]{1,0:T(8,128)(2,1)S(1)}, f32[1024,128]{1,0:T(8,128)S(1)}, bf16[4,128,2176]{2,1,0:T(8,128)(2,1)S(1)}) custom-call(s32[5]{0:T(128)S(1)} %stack.23.place, bf16[384,3072]{1,0:T(8,128)(2,1)S(1)} %get-tuple-element.119.packed_grad, bf16[1024,3072]{1,0:T(8,128)(2,1)S(1)} %bitcast.8, ...), custom_call_target="tpu_custom_call" | custom-call | tf_op jit(solution)/shard_map/norm/pallas_call | solution.py:56
  65.4 2.4 %keep_left.1 = (f32[128,3072]{1,0:T(8,128)S(1)}, bf16[128,3072]{1,0:T(8,128)(2,1)S(1)}, bf16[128,3072]{1,0:T(8,128)(2,1)S(1)}, bf16[128,3072]{1,0:T(8,128)(2,1)S(1)}) custom-call(s32[5]{0:T(128)S(1)} %stack.23.place, bf16[384,1024]{1,0:T(8,128)(2,1)S(1)} %get-tuple-element.118.normed, bf16[384,3072]{1,0:T(8,128)(2,1)S(1)} %get-tuple-element.119.packed_grad, ...), custom_call_target="tpu_custom_call" | custom-call | tf_op jit(solution)/shard_map/keep_left/pallas_call | solution.py:56
  67.8 4.4 %collective-permute-start.15 = (bf16[128,3072]{1,0:T(8,128)(2,1)S(1)}, bf16[128,3072]{1,0:T(8,128)(2,1)S(1)}, u32[]{:S(2)}, u32[]{:S(2)}) collective-permute-start(bf16[128,3072]{1,0:T(8,128)(2,1)S(1)} %get-tuple-element.141), channel_id=1, source_target_pairs={{0,96},{32,64},{64,32},{96,0},{1,97},{33,65},{65,33},{97,1},{2,98}... | collective-permute-start | bytes 2359304 | tf_op jit(solution)/shard_map/ppermute | solution.py:499
  72.2 1.5 collective-permute-start.12
  73.7 1.7 %collective-permute-start.11 = (bf16[96,1152]{1,0:T(8,128)(2,1)S(1)}, bf16[96,1152]{1,0:T(8,128)(2,1)S(1)}, u32[]{:S(2)}, u32[]{:S(2)}) collective-permute-start(bf16[96,1152]{1,0:T(8,128)(2,1)S(1)} %get-tuple-element.127.m0), channel_id=1, source_target_pairs={{0,8},{4,12},{8,0},{12,4},{1,9},{5,13},{9,1},{13,5},{2,10},{6,14},... | collective-permute-start | bytes 663560 | tf_op jit(solution)/shard_map/ppermute | solution.py:499
  76.3 2.2 %keep_right.1 = (f32[4,32,2176]{2,1,0:T(8,128)S(1)}, bf16[4,32,2176]{2,1,0:T(8,128)(2,1)S(1)}, bf16[4,32,2176]{2,1,0:T(8,128)(2,1)S(1)}, bf16[4,32,2176]{2,1,0:T(8,128)(2,1)S(1)}) custom-call(s32[5]{0:T(128)S(1)} %stack.23.place, bf16[384,1024]{1,0:T(8,128)(2,1)S(1)} %get-tuple-element.125.mixed, bf16[384,1024]{1,0:T(8,128)(2,1)S(1)} %get-tuple-element.126.grad_low, ...), custom_call_target="tpu_custom_call" | custom-call | tf_op jit(solution)/shard_map/keep_right/pallas_call | solution.py:56
  78.5 5.5 %collective-permute-done.12.m3 = bf16[96,1152]{1,0:T(8,128)(2,1)S(1)} collective-permute-done((bf16[96,1152]{1,0:T(8,128)(2,1)S(1)}, bf16[96,1152]{1,0:T(8,128)(2,1)S(1)}, u32[]{:S(2)}, u32[]{:S(2)}) %collective-permute-start.12) | collective-permute-done | bytes 221216 | tf_op jit(solution)/shard_map/ppermute | solution.py:499
  84.0 1.5 collective-permute-start.17
  85.5 2.8 %collective-permute-start.16 = (bf16[4,32,2176]{2,1,0:T(8,128)(2,1)S(1)}, bf16[4,32,2176]{2,1,0:T(8,128)(2,1)S(1)}, u32[]{:S(2)}, u32[]{:S(2)}) collective-permute-start(bf16[4,32,2176]{2,1,0:T(8,128)(2,1)S(1)} %get-tuple-element.138), channel_id=1, source_target_pairs={{0,4},{4,0},{8,12},{12,8},{1,5},{5,1},{9,13},{13,9},{2,6},{6,2},{1... | collective-permute-start | bytes 1671176 | tf_op jit(solution)/shard_map/ppermute | solution.py:499
  88.3 3.7 %table.3 = (bf16[4,32,2048]{2,1,0:T(8,128)(2,1)S(1)}, f32[4,32,2048]{2,1,0:T(8,128)S(1)}) custom-call(s32[5]{0:T(128)S(1)} %stack.23.place, bf16[96,1152]{1,0:T(8,128)(2,1)S(1)} %get-tuple-element.127.m0, bf16[96,1152]{1,0:T(8,128)(2,1)S(1)} %collective-permute-done.10.m1, bf16[96,1152]{1,0:T(8,128)(2,1)S(1)} %collective-permute-done.11.m2, ...), custom_call_target="tpu_custom_call" | custom-call | tf_op jit(solution)/shard_map/table/pallas_call | solution.py:56
  92.2 1.8 %collective-permute-done.13.got = bf16[4,32,2048]{2,1,0:T(8,128)(2,1)S(1)} collective-permute-done((bf16[4,32,2048]{2,1,0:T(8,128)(2,1)S(1)}, bf16[4,32,2048]{2,1,0:T(8,128)(2,1)S(1)}, u32[]{:S(2)}, u32[]{:S(2)}) %collective-permute-start.13) | collective-permute-done | bytes 524320 | tf_op jit(solution)/shard_map/ppermute | solution.py:499
  94.0 3.2 %collective-permute-done.17.g3 = bf16[4,32,2176]{2,1,0:T(8,128)(2,1)S(1)} collective-permute-done((bf16[4,32,2176]{2,1,0:T(8,128)(2,1)S(1)}, bf16[4,32,2176]{2,1,0:T(8,128)(2,1)S(1)}, u32[]{:S(2)}, u32[]{:S(2)}) %collective-permute-start.17) | collective-permute-done | bytes 557088 | tf_op jit(solution)/shard_map/ppermute | solution.py:499
  97.2 2.5 %collective-permute-done.16.g1 = bf16[4,32,2176]{2,1,0:T(8,128)(2,1)S(1)} collective-permute-done((bf16[4,32,2176]{2,1,0:T(8,128)(2,1)S(1)}, bf16[4,32,2176]{2,1,0:T(8,128)(2,1)S(1)}, u32[]{:S(2)}, u32[]{:S(2)}) %collective-permute-start.16) | collective-permute-done | bytes 557088 | tf_op jit(solution)/shard_map/ppermute | solution.py:499
  99.7 1.6 %collective-permute-start.18 = (bf16[128,3072]{1,0:T(8,128)(2,1)S(1)}, bf16[128,3072]{1,0:T(8,128)(2,1)S(1)}, u32[]{:S(2)}, u32[]{:S(2)}) collective-permute-start(bf16[128,3072]{1,0:T(8,128)(2,1)S(1)} %get-tuple-element.144), channel_id=1, source_target_pairs={{0,64},{32,96},{64,0},{96,32},{1,65},{33,97},{65,1},{97,33},{2,66}... | collective-permute-start | bytes 2359304 | tf_op jit(solution)/shard_map/ppermute | solution.py:499
  101.2 2.1 %collective-permute-start.22 = (bf16[4,32,2176]{2,1,0:T(8,128)(2,1)S(1)}, bf16[4,32,2176]{2,1,0:T(8,128)(2,1)S(1)}, u32[]{:S(2)}, u32[]{:S(2)}) collective-permute-start(bf16[4,32,2176]{2,1,0:T(8,128)(2,1)S(1)} %get-tuple-element.152), channel_id=1, source_target_pairs={{0,8},{4,12},{8,0},{12,4},{1,9},{5,13},{9,1},{13,5},{2,10},{6,14},... | collective-permute-start | bytes 1671176 | tf_op jit(solution)/shard_map/ppermute | solution.py:499
  103.4 2.2 %collective-permute-start.28 = (bf16[192,1024]{1,0:T(8,128)(2,1)S(1)}, bf16[192,1024]{1,0:T(8,128)(2,1)S(1)}, u32[]{:S(2)}, u32[]{:S(2)}) collective-permute-start(bf16[192,1024]{1,0:T(8,128)(2,1)S(1)} %pad_maximum_fusion.p0), channel_id=1, source_target_pairs={{0,3},{1,2},{2,1},{3,0},{4,7},{5,6},{6,5},{7,4},{8,11},{9,10},{10,... | collective-permute-start | bytes 1179656 | tf_op jit(solution)/shard_map/ppermute | solution.py:499
  105.6 1.9 %collective-permute-start.26 = (bf16[192,1024]{1,0:T(8,128)(2,1)S(1)}, bf16[192,1024]{1,0:T(8,128)(2,1)S(1)}, u32[]{:S(2)}, u32[]{:S(2)}) collective-permute-start(bf16[192,1024]{1,0:T(8,128)(2,1)S(1)} %pad_maximum_fusion.p0), channel_id=1, source_target_pairs={{0,1},{1,0},{2,3},{3,2},{4,5},{5,4},{6,7},{7,6},{8,9},{9,8},{10,11... | collective-permute-start | bytes 1179656 | tf_op jit(solution)/shard_map/ppermute | solution.py:499
  107.5 7.5 %collective-permute-done.22.g2 = bf16[4,32,2176]{2,1,0:T(8,128)(2,1)S(1)} collective-permute-done((bf16[4,32,2176]{2,1,0:T(8,128)(2,1)S(1)}, bf16[4,32,2176]{2,1,0:T(8,128)(2,1)S(1)}, u32[]{:S(2)}, u32[]{:S(2)}) %collective-permute-start.22) | collective-permute-done | bytes 557088 | tf_op jit(solution)/shard_map/ppermute | solution.py:499
  116.0 5.4 %collective-permute-done.28.p3 = bf16[192,1024]{1,0:T(8,128)(2,1)S(1)} collective-permute-done((bf16[192,1024]{1,0:T(8,128)(2,1)S(1)}, bf16[192,1024]{1,0:T(8,128)(2,1)S(1)}, u32[]{:S(2)}, u32[]{:S(2)}) %collective-permute-start.28) | collective-permute-done | bytes 393248 | tf_op jit(solution)/shard_map/ppermute | solution.py:499
  122.0 1.7 %win.1 = (bf16[4,256,128]{2,1,0:T(8,128)(2,1)S(1)}, f32[4,256,128]{2,1,0:T(8,128)S(1)}) custom-call(s32[5]{0:T(128)S(1)} %stack.23.place, bf16[192,1024]{1,0:T(8,128)(2,1)S(1)} %pad_maximum_fusion.p0, bf16[192,1024]{1,0:T(8,128)(2,1)S(1)} %collective-permute-done.26.p1, bf16[192,1024]{1,0:T(8,128)(2,1)S(1)} %collective-permute-done.27.p2, ...), custom_call_target="tpu_custom_call" | custom-call | tf_op jit(solution)/shard_map/win/pallas_call | solution.py:56
  123.9 2.1 %collective-permute-start.24 = (bf16[32,4224]{1,0:T(8,128)(2,1)S(1)}, bf16[32,4224]{1,0:T(8,128)(2,1)S(1)}, u32[]{:S(2)}, u32[]{:S(2)}) collective-permute-start(bf16[32,4224]{1,0:T(8,128)(2,1)S(1)} %get-tuple-element.158), channel_id=1, source_target_pairs={{0,64},{32,96},{64,0},{96,32},{1,65},{33,97},{65,1},{97,33},{2,66}... | collective-permute-start | bytes 811016 | tf_op jit(solution)/shard_map/ppermute | solution.py:499
  128.1 2.2 %collective-permute-start.20 = (bf16[32,3072]{1,0:T(8,128)(2,1)S(1)}, bf16[32,3072]{1,0:T(8,128)(2,1)S(1)}, u32[]{:S(2)}, u32[]{:S(2)}) collective-permute-start(bf16[32,3072]{1,0:T(8,128)(2,1)S(1)} %get-tuple-element.148), channel_id=1, source_target_pairs={{0,8},{4,12},{8,0},{12,4},{1,9},{5,13},{9,1},{13,5},{2,10},{6,14},... | collective-permute-start | bytes 589832 | tf_op jit(solution)/shard_map/ppermute | solution.py:499
  132.1 2.2 %collective-permute-done.24.r2 = bf16[32,4224]{1,0:T(8,128)(2,1)S(1)} collective-permute-done((bf16[32,4224]{1,0:T(8,128)(2,1)S(1)}, bf16[32,4224]{1,0:T(8,128)(2,1)S(1)}, u32[]{:S(2)}, u32[]{:S(2)}) %collective-permute-start.24) | collective-permute-done | bytes 270368 | tf_op jit(solution)/shard_map/ppermute | solution.py:499
  134.5 5.6 %collective-permute-done.25.r3 = bf16[32,4224]{1,0:T(8,128)(2,1)S(1)} collective-permute-done((bf16[32,4224]{1,0:T(8,128)(2,1)S(1)}, bf16[32,4224]{1,0:T(8,128)(2,1)S(1)}, u32[]{:S(2)}, u32[]{:S(2)}) %collective-permute-start.25) | collective-permute-done | bytes 270368 | tf_op jit(solution)/shard_map/ppermute | solution.py:499
  140.1 1.8 %collective-permute-start.31 = (bf16[256,128]{1,0:T(8,128)(2,1)S(1)}, bf16[256,128]{1,0:T(8,128)(2,1)S(1)}, u32[]{:S(2)}, u32[]{:S(2)}) collective-permute-start(bf16[256,128]{1,0:T(8,128)(2,1)S(1)} %get-tuple-element.169), channel_id=1, source_target_pairs={{0,64},{32,96},{64,0},{96,32},{1,65},{33,97},{65,1},{97,33},{2,66}... | collective-permute-start | bytes 196616 | tf_op jit(solution)/shard_map/ppermute | solution.py:499
  143.8 1.8 %collective-permute-start.34 = (bf16[16,3712]{1,0:T(8,128)(2,1)S(1)}, bf16[16,3712]{1,0:T(8,128)(2,1)S(1)}, u32[]{:S(2)}, u32[]{:S(2)}) collective-permute-start(bf16[16,3712]{1,0:T(8,128)(2,1)S(1)} %get-tuple-element.172), channel_id=1, source_target_pairs={{0,2},{1,3},{2,0},{3,1},{4,6},{5,7},{6,4},{7,5},{8,10},{9,11},{10,... | collective-permute-start | bytes 356360 | tf_op jit(solution)/shard_map/ppermute | solution.py:499
  148.1 2.8 %temporal.3 = bf16[1536,256]{1,0:T(8,128)(2,1)} custom-call(s32[5]{0:T(128)S(1)} %stack.23.place, s32[16,96]{1,0:T(8,128)S(1)} %get-tuple-element.162.keeps, s32[16,96]{1,0:T(8,128)S(1)} %get-tuple-element.163.goes, bf16[192,1024]{1,0:T(8,128)(2,1)S(1)} %pad_maximum_fusion.p0, bf16[192,1024]{1,0:T(8,128)(2,1)S(1)} %collective-permute-done.26.p1, ...), custom_call_target="tpu_custom_call" | custom-call | tf_op jit(solution)/shard_map/temporal/pallas_call | solution.py:56
  150.9 1.6 %collective-permute-done.35.d = bf16[16,3712]{1,0:T(8,128)(2,1)S(1)} collective-permute-done((bf16[16,3712]{1,0:T(8,128)(2,1)S(1)}, bf16[16,3712]{1,0:T(8,128)(2,1)S(1)}, u32[]{:S(2)}, u32[]{:S(2)}) %collective-permute-start.35) | collective-permute-done | bytes 118816 | tf_op jit(solution)/shard_map/ppermute | solution.py:499
  (75 shorter events, 18.5 us)
Async XLA Ops:
  0.6 22.9 %copy-start = (bf16[8,128,1024]{2,1,0:T(8,128)(2,1)S(1)}, bf16[8,128,1024]{2,1,0:T(8,128)(2,1)}, u32[]{:S(2)}) copy-start(bf16[8,128,1024]{2,1,0:T(8,128)(2,1)} %adapter_b.3) | copy-start | bytes 6291460
  2.4 1.0 copy-start.4
  3.5 1.1 copy-start.7
  6.2 10.9 %collective-permute-start.1 = (bf16[192,1024]{1,0:T(8,128)(2,1)S(1)}, bf16[192,1024]{1,0:T(8,128)(2,1)S(1)}, u32[]{:S(2)}, u32[]{:S(2)}) collective-permute-start(bf16[192,1024]{1,0:T(8,128)(2,1)S(1)} %get-tuple-element.97), channel_id=1, source_target_pairs={{0,1},{1,0},{2,3},{3,2},{4,5},{5,4},{6,7},{7,6},{8,9},{9,8},{10,11... | collective-permute-start | bytes 1179656 | tf_op jit(solution)/shard_map/ppermute | solution.py:499
  7.9 11.8 %collective-permute-start.2 = (bf16[192,1024]{1,0:T(8,128)(2,1)S(1)}, bf16[192,1024]{1,0:T(8,128)(2,1)S(1)}, u32[]{:S(2)}, u32[]{:S(2)}) collective-permute-start(bf16[192,1024]{1,0:T(8,128)(2,1)S(1)} %get-tuple-element.98), channel_id=1, source_target_pairs={{0,3},{1,2},{2,1},{3,0},{4,7},{5,6},{6,5},{7,4},{8,11},{9,10},{10,... | collective-permute-start | bytes 1179656 | tf_op jit(solution)/shard_map/ppermute | solution.py:499
  10.1 5.3 %collective-permute-start = (s32[40,8]{1,0:T(8,128)S(1)}, s32[40,8]{1,0:T(8,128)S(1)}, u32[]{:S(2)}, u32[]{:S(2)}) collective-permute-start(s32[40,8]{1,0:T(8,128)S(1)} %get-tuple-element.96), channel_id=1, source_target_pairs={{0,8},{4,12},{8,0},{12,4},{1,9},{5,13},{9,1},{13,5},{2,10},{6,14},... | collective-permute-start | bytes 3848 | tf_op jit(solution)/shard_map/ppermute | solution.py:499
  12.2 1.4 copy-start.1
  19.7 23.3 %slice-start = ((s8[6291456]{0:T(1024)(128)(4,1)}), s8[4194304]{0:T(1024)(128)(4,1)S(1)}, s32[]{:S(2)}) async-start(s8[6291456]{0:T(1024)(128)(4,1)} %bitcast.7), calls=%async_computation | async-start | bytes 8388608
  19.7 23.3 %slice-start.1 = ((s8[6291456]{0:T(1024)(128)(4,1)}), s8[2097152]{0:T(1024)(128)(4,1)S(1)}, s32[]{:S(2)}) async-start(s8[6291456]{0:T(1024)(128)(4,1)} %bitcast.7), calls=%async_computation.1 | async-start | bytes 4194304
  19.7 19.0 %collective-permute-start.7 = (bf16[320,1024]{1,0:T(8,128)(2,1)S(1)}, bf16[320,1024]{1,0:T(8,128)(2,1)S(1)}, u32[]{:S(2)}, u32[]{:S(2)}) collective-permute-start(bf16[320,1024]{1,0:T(8,128)(2,1)S(1)} %leave.1), channel_id=1, source_target_pairs={{0,8},{4,12},{8,0},{12,4},{1,9},{5,13},{9,1},{13,5},{2,10},{6,14},... | collective-permute-start | bytes 1966088 | tf_op jit(solution)/shard_map/ppermute | solution.py:499
  21.8 10.9 %collective-permute-start.3 = (bf16[192,1024]{1,0:T(8,128)(2,1)S(1)}, bf16[192,1024]{1,0:T(8,128)(2,1)S(1)}, u32[]{:S(2)}, u32[]{:S(2)}) collective-permute-start(bf16[192,1024]{1,0:T(8,128)(2,1)S(1)} %get-tuple-element.105), channel_id=1, source_target_pairs={{0,2},{1,3},{2,0},{3,1},{4,6},{5,7},{6,4},{7,5},{8,10},{9,11},{10,... | collective-permute-start | bytes 1179656 | tf_op jit(solution)/shard_map/ppermute | solution.py:499
  23.5 2.2 %copy-start.3 = (bf16[8,2048,128]{2,1,0:T(8,128)(2,1)S(1)}, bf16[8,2048,128]{2,1,0:T(8,128)(2,1)}, u32[]{:S(2)}) copy-start(bf16[8,2048,128]{2,1,0:T(8,128)(2,1)} %table.2) | copy-start | bytes 12582916
  28.5 10.1 %copy-start.2 = (bf16[96,8,1024]{2,1,0:T(8,128)(2,1)S(1)}, bf16[96,8,1024]{2,1,0:T(8,128)(2,1)}, u32[]{:S(2)}) copy-start(bf16[96,8,1024]{2,1,0:T(8,128)(2,1)} %param.15) | copy-start | bytes 4718596
  33.5 9.5 %copy-start.8 = (f32[1024]{0:T(1024)S(1)}, f32[1024]{0:T(1024)}, u32[]{:S(2)}) copy-start(f32[1024]{0:T(1024)} %param.16) | copy-start | bytes 12292
  33.6 9.4 %collective-permute-start.4 = (bf16[48,1024]{1,0:T(8,128)(2,1)S(1)}, bf16[48,1024]{1,0:T(8,128)(2,1)S(1)}, u32[]{:S(2)}, u32[]{:S(2)}) collective-permute-start(bf16[48,1024]{1,0:T(8,128)(2,1)S(1)} %get-tuple-element.108), channel_id=1, source_target_pairs={{0,4},{4,0},{8,12},{12,8},{1,5},{5,1},{9,13},{13,9},{2,6},{6,2},{1... | collective-permute-start | bytes 294920 | tf_op jit(solution)/shard_map/ppermute | solution.py:499
  35.1 7.9 %collective-permute-start.5 = (bf16[48,1024]{1,0:T(8,128)(2,1)S(1)}, bf16[48,1024]{1,0:T(8,128)(2,1)S(1)}, u32[]{:S(2)}, u32[]{:S(2)}) collective-permute-start(bf16[48,1024]{1,0:T(8,128)(2,1)S(1)} %get-tuple-element.109), channel_id=1, source_target_pairs={{0,8},{4,12},{8,0},{12,4},{1,9},{5,13},{9,1},{13,5},{2,10},{6,14},... | collective-permute-start | bytes 294920 | tf_op jit(solution)/shard_map/ppermute | solution.py:499
  35.1 7.9 %collective-permute-start.6 = (bf16[48,1024]{1,0:T(8,128)(2,1)S(1)}, bf16[48,1024]{1,0:T(8,128)(2,1)S(1)}, u32[]{:S(2)}, u32[]{:S(2)}) collective-permute-start(bf16[48,1024]{1,0:T(8,128)(2,1)S(1)} %get-tuple-element.110), channel_id=1, source_target_pairs={{0,12},{4,8},{8,4},{12,0},{1,13},{5,9},{9,5},{13,1},{2,14},{6,10},... | collective-permute-start | bytes 294920 | tf_op jit(solution)/shard_map/ppermute | solution.py:499
  38.7 1.6 %copy-start.6 = (bf16[1024,1024]{1,0:T(8,128)(2,1)S(1)}, bf16[1024,1024]{1,0:T(8,128)(2,1)}, u32[]{:S(2)}) copy-start(bf16[1024,1024]{1,0:T(8,128)(2,1)} %w_out.1) | copy-start | bytes 6291460
  58.1 7.3 %collective-permute-start.8 = (bf16[4,128,3072]{2,1,0:T(8,128)(2,1)S(1)}, bf16[4,128,3072]{2,1,0:T(8,128)(2,1)S(1)}, u32[]{:S(2)}, u32[]{:S(2)}) collective-permute-start(bf16[4,128,3072]{2,1,0:T(8,128)(2,1)S(1)} %get-tuple-element.129), channel_id=1, source_target_pairs={{0,16},{16,0},{1,17},{17,1},{2,18},{18,2},{3,19},{19,3},{4,20},{20... | collective-permute-start | bytes 9437192 | tf_op jit(solution)/shard_map/ppermute | solution.py:499
  64.9 10.5 %collective-permute-start.9 = (bf16[4,128,2176]{2,1,0:T(8,128)(2,1)S(1)}, bf16[4,128,2176]{2,1,0:T(8,128)(2,1)S(1)}, u32[]{:S(2)}, u32[]{:S(2)}) collective-permute-start(bf16[4,128,2176]{2,1,0:T(8,128)(2,1)S(1)} %get-tuple-element.136), channel_id=1, source_target_pairs={{0,16},{16,0},{1,17},{17,1},{2,18},{18,2},{3,19},{19,3},{4,20},{20... | collective-permute-start | bytes 6684680 | tf_op jit(solution)/shard_map/ppermute | solution.py:499
  67.8 31.8 %collective-permute-start.15 = (bf16[128,3072]{1,0:T(8,128)(2,1)S(1)}, bf16[128,3072]{1,0:T(8,128)(2,1)S(1)}, u32[]{:S(2)}, u32[]{:S(2)}) collective-permute-start(bf16[128,3072]{1,0:T(8,128)(2,1)S(1)} %get-tuple-element.141), channel_id=1, source_target_pairs={{0,96},{32,64},{64,32},{96,0},{1,97},{33,65},{65,33},{97,1},{2,98}... | collective-permute-start | bytes 2359304 | tf_op jit(solution)/shard_map/ppermute | solution.py:499
  72.2 27.5 %collective-permute-start.14 = (bf16[128,3072]{1,0:T(8,128)(2,1)S(1)}, bf16[128,3072]{1,0:T(8,128)(2,1)S(1)}, u32[]{:S(2)}, u32[]{:S(2)}) collective-permute-start(bf16[128,3072]{1,0:T(8,128)(2,1)S(1)} %get-tuple-element.132), channel_id=1, source_target_pairs={{0,32},{32,0},{64,96},{96,64},{1,33},{33,1},{65,97},{97,65},{2,34}... | collective-permute-start | bytes 2359304 | tf_op jit(solution)/shard_map/ppermute | solution.py:499
  72.2 11.8 %collective-permute-start.12 = (bf16[96,1152]{1,0:T(8,128)(2,1)S(1)}, bf16[96,1152]{1,0:T(8,128)(2,1)S(1)}, u32[]{:S(2)}, u32[]{:S(2)}) collective-permute-start(bf16[96,1152]{1,0:T(8,128)(2,1)S(1)} %get-tuple-element.127.m0), channel_id=1, source_target_pairs={{0,12},{4,8},{8,4},{12,0},{1,13},{5,9},{9,5},{13,1},{2,14},{6,10},... | collective-permute-start | bytes 663560 | tf_op jit(solution)/shard_map/ppermute | solution.py:499
  73.7 11.8 %collective-permute-start.11 = (bf16[96,1152]{1,0:T(8,128)(2,1)S(1)}, bf16[96,1152]{1,0:T(8,128)(2,1)S(1)}, u32[]{:S(2)}, u32[]{:S(2)}) collective-permute-start(bf16[96,1152]{1,0:T(8,128)(2,1)S(1)} %get-tuple-element.127.m0), channel_id=1, source_target_pairs={{0,8},{4,12},{8,0},{12,4},{1,9},{5,13},{9,1},{13,5},{2,10},{6,14},... | collective-permute-start | bytes 663560 | tf_op jit(solution)/shard_map/ppermute | solution.py:499
  75.4 12.9 %collective-permute-start.10 = (bf16[96,1152]{1,0:T(8,128)(2,1)S(1)}, bf16[96,1152]{1,0:T(8,128)(2,1)S(1)}, u32[]{:S(2)}, u32[]{:S(2)}) collective-permute-start(bf16[96,1152]{1,0:T(8,128)(2,1)S(1)} %get-tuple-element.127.m0), channel_id=1, source_target_pairs={{0,4},{4,0},{8,12},{12,8},{1,5},{5,1},{9,13},{13,9},{2,6},{6,2},{1... | collective-permute-start | bytes 663560 | tf_op jit(solution)/shard_map/ppermute | solution.py:499
  84.0 13.2 %collective-permute-start.17 = (bf16[4,32,2176]{2,1,0:T(8,128)(2,1)S(1)}, bf16[4,32,2176]{2,1,0:T(8,128)(2,1)S(1)}, u32[]{:S(2)}, u32[]{:S(2)}) collective-permute-start(bf16[4,32,2176]{2,1,0:T(8,128)(2,1)S(1)} %get-tuple-element.142), channel_id=1, source_target_pairs={{0,12},{4,8},{8,4},{12,0},{1,13},{5,9},{9,5},{13,1},{2,14},{6,10},... | collective-permute-start | bytes 1671176 | tf_op jit(solution)/shard_map/ppermute | solution.py:499
  85.5 14.1 %collective-permute-start.16 = (bf16[4,32,2176]{2,1,0:T(8,128)(2,1)S(1)}, bf16[4,32,2176]{2,1,0:T(8,128)(2,1)S(1)}, u32[]{:S(2)}, u32[]{:S(2)}) collective-permute-start(bf16[4,32,2176]{2,1,0:T(8,128)(2,1)S(1)} %get-tuple-element.138), channel_id=1, source_target_pairs={{0,4},{4,0},{8,12},{12,8},{1,5},{5,1},{9,13},{13,9},{2,6},{6,2},{1... | collective-permute-start | bytes 1671176 | tf_op jit(solution)/shard_map/ppermute | solution.py:499
  92.0 2.0 %collective-permute-start.13 = (bf16[4,32,2048]{2,1,0:T(8,128)(2,1)S(1)}, bf16[4,32,2048]{2,1,0:T(8,128)(2,1)S(1)}, u32[]{:S(2)}, u32[]{:S(2)}) collective-permute-start(bf16[4,32,2048]{2,1,0:T(8,128)(2,1)S(1)} %get-tuple-element.140), channel_id=1, source_target_pairs={{0,16},{16,0},{1,17},{17,1},{2,18},{18,2},{3,19},{19,3},{4,20},{20... | collective-permute-start | bytes 1572872 | tf_op jit(solution)/shard_map/ppermute | solution.py:499
  99.7 27.1 %collective-permute-start.18 = (bf16[128,3072]{1,0:T(8,128)(2,1)S(1)}, bf16[128,3072]{1,0:T(8,128)(2,1)S(1)}, u32[]{:S(2)}, u32[]{:S(2)}) collective-permute-start(bf16[128,3072]{1,0:T(8,128)(2,1)S(1)} %get-tuple-element.144), channel_id=1, source_target_pairs={{0,64},{32,96},{64,0},{96,32},{1,65},{33,97},{65,1},{97,33},{2,66}... | collective-permute-start | bytes 2359304 | tf_op jit(solution)/shard_map/ppermute | solution.py:499
  101.2 13.7 %collective-permute-start.22 = (bf16[4,32,2176]{2,1,0:T(8,128)(2,1)S(1)}, bf16[4,32,2176]{2,1,0:T(8,128)(2,1)S(1)}, u32[]{:S(2)}, u32[]{:S(2)}) collective-permute-start(bf16[4,32,2176]{2,1,0:T(8,128)(2,1)S(1)} %get-tuple-element.152), channel_id=1, source_target_pairs={{0,8},{4,12},{8,0},{12,4},{1,9},{5,13},{9,1},{13,5},{2,10},{6,14},... | collective-permute-start | bytes 1671176 | tf_op jit(solution)/shard_map/ppermute | solution.py:499
  103.4 18.0 %collective-permute-start.28 = (bf16[192,1024]{1,0:T(8,128)(2,1)S(1)}, bf16[192,1024]{1,0:T(8,128)(2,1)S(1)}, u32[]{:S(2)}, u32[]{:S(2)}) collective-permute-start(bf16[192,1024]{1,0:T(8,128)(2,1)S(1)} %pad_maximum_fusion.p0), channel_id=1, source_target_pairs={{0,3},{1,2},{2,1},{3,0},{4,7},{5,6},{6,5},{7,4},{8,11},{9,10},{10,... | collective-permute-start | bytes 1179656 | tf_op jit(solution)/shard_map/ppermute | solution.py:499
  105.6 15.9 %collective-permute-start.27 = (bf16[192,1024]{1,0:T(8,128)(2,1)S(1)}, bf16[192,1024]{1,0:T(8,128)(2,1)S(1)}, u32[]{:S(2)}, u32[]{:S(2)}) collective-permute-start(bf16[192,1024]{1,0:T(8,128)(2,1)S(1)} %pad_maximum_fusion.p0), channel_id=1, source_target_pairs={{0,2},{1,3},{2,0},{3,1},{4,6},{5,7},{6,4},{7,5},{8,10},{9,11},{10,... | collective-permute-start | bytes 1179656 | tf_op jit(solution)/shard_map/ppermute | solution.py:499
  105.6 16.5 %collective-permute-start.26 = (bf16[192,1024]{1,0:T(8,128)(2,1)S(1)}, bf16[192,1024]{1,0:T(8,128)(2,1)S(1)}, u32[]{:S(2)}, u32[]{:S(2)}) collective-permute-start(bf16[192,1024]{1,0:T(8,128)(2,1)S(1)} %pad_maximum_fusion.p0), channel_id=1, source_target_pairs={{0,1},{1,0},{2,3},{3,2},{4,5},{5,4},{6,7},{7,6},{8,9},{9,8},{10,11... | collective-permute-start | bytes 1179656 | tf_op jit(solution)/shard_map/ppermute | solution.py:499
  115.8 14.5 %collective-permute-start.23 = (bf16[32,4224]{1,0:T(8,128)(2,1)S(1)}, bf16[32,4224]{1,0:T(8,128)(2,1)S(1)}, u32[]{:S(2)}, u32[]{:S(2)}) collective-permute-start(bf16[32,4224]{1,0:T(8,128)(2,1)S(1)} %get-tuple-element.157), channel_id=1, source_target_pairs={{0,32},{32,0},{64,96},{96,64},{1,33},{33,1},{65,97},{97,65},{2,34}... | collective-permute-start | bytes 811016 | tf_op jit(solution)/shard_map/ppermute | solution.py:499
  123.8 4.3 %collective-permute-start.29 = (bf16[4,256,128]{2,1,0:T(8,128)(2,1)S(1)}, bf16[4,256,128]{2,1,0:T(8,128)(2,1)S(1)}, u32[]{:S(2)}, u32[]{:S(2)}) collective-permute-start(bf16[4,256,128]{2,1,0:T(8,128)(2,1)S(1)} %get-tuple-element.166), channel_id=1, source_target_pairs={{0,16},{16,0},{1,17},{17,1},{2,18},{18,2},{3,19},{19,3},{4,20},{20... | collective-permute-start | bytes 786440 | tf_op jit(solution)/shard_map/ppermute | solution.py:499
  123.9 10.5 %collective-permute-start.24 = (bf16[32,4224]{1,0:T(8,128)(2,1)S(1)}, bf16[32,4224]{1,0:T(8,128)(2,1)S(1)}, u32[]{:S(2)}, u32[]{:S(2)}) collective-permute-start(bf16[32,4224]{1,0:T(8,128)(2,1)S(1)} %get-tuple-element.158), channel_id=1, source_target_pairs={{0,64},{32,96},{64,0},{96,32},{1,65},{33,97},{65,1},{97,33},{2,66}... | collective-permute-start | bytes 811016 | tf_op jit(solution)/shard_map/ppermute | solution.py:499
  125.9 14.1 %collective-permute-start.25 = (bf16[32,4224]{1,0:T(8,128)(2,1)S(1)}, bf16[32,4224]{1,0:T(8,128)(2,1)S(1)}, u32[]{:S(2)}, u32[]{:S(2)}) collective-permute-start(bf16[32,4224]{1,0:T(8,128)(2,1)S(1)} %get-tuple-element.159), channel_id=1, source_target_pairs={{0,96},{32,64},{64,32},{96,0},{1,97},{33,65},{65,33},{97,1},{2,98}... | collective-permute-start | bytes 811016 | tf_op jit(solution)/shard_map/ppermute | solution.py:499
  127.9 20.1 %copy-start.5 = (bf16[256,1024]{1,0:T(8,128)(2,1)S(1)}, bf16[256,1024]{1,0:T(8,128)(2,1)}, u32[]{:S(2)}) copy-start(bf16[256,1024]{1,0:T(8,128)(2,1)} %w_in.3) | copy-start | bytes 1572868
  127.9 13.9 %collective-permute-start.19 = (bf16[32,3072]{1,0:T(8,128)(2,1)S(1)}, bf16[32,3072]{1,0:T(8,128)(2,1)S(1)}, u32[]{:S(2)}, u32[]{:S(2)}) collective-permute-start(bf16[32,3072]{1,0:T(8,128)(2,1)S(1)} %get-tuple-element.147), channel_id=1, source_target_pairs={{0,4},{4,0},{8,12},{12,8},{1,5},{5,1},{9,13},{13,9},{2,6},{6,2},{1... | collective-permute-start | bytes 589832 | tf_op jit(solution)/shard_map/ppermute | solution.py:499
  128.1 14.8 %collective-permute-start.20 = (bf16[32,3072]{1,0:T(8,128)(2,1)S(1)}, bf16[32,3072]{1,0:T(8,128)(2,1)S(1)}, u32[]{:S(2)}, u32[]{:S(2)}) collective-permute-start(bf16[32,3072]{1,0:T(8,128)(2,1)S(1)} %get-tuple-element.148), channel_id=1, source_target_pairs={{0,8},{4,12},{8,0},{12,4},{1,9},{5,13},{9,1},{13,5},{2,10},{6,14},... | collective-permute-start | bytes 589832 | tf_op jit(solution)/shard_map/ppermute | solution.py:499
  130.3 12.6 %collective-permute-start.21 = (bf16[32,3072]{1,0:T(8,128)(2,1)S(1)}, bf16[32,3072]{1,0:T(8,128)(2,1)S(1)}, u32[]{:S(2)}, u32[]{:S(2)}) collective-permute-start(bf16[32,3072]{1,0:T(8,128)(2,1)S(1)} %get-tuple-element.149), channel_id=1, source_target_pairs={{0,12},{4,8},{8,4},{12,0},{1,13},{5,9},{9,5},{13,1},{2,14},{6,10},... | collective-permute-start | bytes 589832 | tf_op jit(solution)/shard_map/ppermute | solution.py:499
  134.4 12.6 %collective-permute-start.30 = (bf16[256,128]{1,0:T(8,128)(2,1)S(1)}, bf16[256,128]{1,0:T(8,128)(2,1)S(1)}, u32[]{:S(2)}, u32[]{:S(2)}) collective-permute-start(bf16[256,128]{1,0:T(8,128)(2,1)S(1)} %get-tuple-element.168), channel_id=1, source_target_pairs={{0,32},{32,0},{64,96},{96,64},{1,33},{33,1},{65,97},{97,65},{2,34}... | collective-permute-start | bytes 196616 | tf_op jit(solution)/shard_map/ppermute | solution.py:499
  140.1 7.3 %collective-permute-start.31 = (bf16[256,128]{1,0:T(8,128)(2,1)S(1)}, bf16[256,128]{1,0:T(8,128)(2,1)S(1)}, u32[]{:S(2)}, u32[]{:S(2)}) collective-permute-start(bf16[256,128]{1,0:T(8,128)(2,1)S(1)} %get-tuple-element.169), channel_id=1, source_target_pairs={{0,64},{32,96},{64,0},{96,32},{1,65},{33,97},{65,1},{97,33},{2,66}... | collective-permute-start | bytes 196616 | tf_op jit(solution)/shard_map/ppermute | solution.py:499
  141.9 5.5 %collective-permute-start.32 = (bf16[256,128]{1,0:T(8,128)(2,1)S(1)}, bf16[256,128]{1,0:T(8,128)(2,1)S(1)}, u32[]{:S(2)}, u32[]{:S(2)}) collective-permute-start(bf16[256,128]{1,0:T(8,128)(2,1)S(1)} %get-tuple-element.170), channel_id=1, source_target_pairs={{0,96},{32,64},{64,32},{96,0},{1,97},{33,65},{65,33},{97,1},{2,98}... | collective-permute-start | bytes 196616 | tf_op jit(solution)/shard_map/ppermute | solution.py:499
  143.8 7.1 %collective-permute-start.34 = (bf16[16,3712]{1,0:T(8,128)(2,1)S(1)}, bf16[16,3712]{1,0:T(8,128)(2,1)S(1)}, u32[]{:S(2)}, u32[]{:S(2)}) collective-permute-start(bf16[16,3712]{1,0:T(8,128)(2,1)S(1)} %get-tuple-element.172), channel_id=1, source_target_pairs={{0,2},{1,3},{2,0},{3,1},{4,6},{5,7},{6,4},{7,5},{8,10},{9,11},{10,... | collective-permute-start | bytes 356360 | tf_op jit(solution)/shard_map/ppermute | solution.py:499
  145.6 6.9 %collective-permute-start.35 = (bf16[16,3712]{1,0:T(8,128)(2,1)S(1)}, bf16[16,3712]{1,0:T(8,128)(2,1)S(1)}, u32[]{:S(2)}, u32[]{:S(2)}) collective-permute-start(bf16[16,3712]{1,0:T(8,128)(2,1)S(1)} %get-tuple-element.173), channel_id=1, source_target_pairs={{0,3},{1,2},{2,1},{3,0},{4,7},{5,6},{6,5},{7,4},{8,11},{9,10},{10,... | collective-permute-start | bytes 356360 | tf_op jit(solution)/shard_map/ppermute | solution.py:499
  146.9 5.6 %collective-permute-start.33 = (bf16[16,3712]{1,0:T(8,128)(2,1)S(1)}, bf16[16,3712]{1,0:T(8,128)(2,1)S(1)}, u32[]{:S(2)}, u32[]{:S(2)}) collective-permute-start(bf16[16,3712]{1,0:T(8,128)(2,1)S(1)} %get-tuple-element.160), channel_id=1, source_target_pairs={{0,1},{1,0},{2,3},{3,2},{4,5},{5,4},{6,7},{7,6},{8,9},{9,8},{10,11... | collective-permute-start | bytes 356360 | tf_op jit(solution)/shard_map/ppermute | solution.py:499

commit v2 on v1

--- a/solution.py
+++ b/solution.py
@@ -220,9 +220,9 @@
     query_row = iota((SPAN, 2 * SPAN), 1) % SPAN
     allowed = (key_row % GROUP == query_row % GROUP) & (key_row // GROUP <= query_row // GROUP)
 
-    @pl.loop(0, HEADS // 8)
+    @pl.loop(0, HEADS // 16)
     def _(half):
-        for p, g in ((half * 4 + i, g) for i in range(4) for g in range(GROUPS)):
+        for p, g in ((half * 8 + i, g) for i in range(8) for g in range(GROUPS)):
             rows = pl.ds(g * SPAN, SPAN)
             query = split(packed_o[rows, pair_columns(0, p)])
             keys = packed_o[rows, pair_columns(1, p)]
@@ -237,9 +237,9 @@
 
 
 def backward_kernel(packed, probs_in, grad_mixed, packed_grad_o):
-    @pl.loop(0, HEADS // 8)
+    @pl.loop(0, HEADS // 16)
     def _(half):
-        for p, g in ((half * 4 + i, g) for i in range(4) for g in range(GROUPS)):
+        for p, g in ((half * 8 + i, g) for i in range(8) for g in range(GROUPS)):
             rows = pl.ds(g * SPAN, SPAN)
             query = split(packed[rows, pair_columns(0, p)])
             keys = packed[rows, pair_columns(1, p)]

time: 154 us -> 153 us (level)
  no operation moved by 1% of the time
where the time goes in v2:
time: 153 us
  starting transfers between devices  47.8 us (31%)
  Pallas kernels  47.6 us (31%)
  waiting for transfers between devices  46.2 us (30%)
  local copies, waits for them, and re-layouts  9.84 us (6%)
    ppermute x36, starting transfers between devices, swap(): return lax.ppermute(x, axis, [(i, i ^ d) for i in range(n)])  47.8 us
    pallas_call x18, Pallas kernels, call(): pl.pallas_call(kernel, out_shape=out, in_specs=[smem] * scalars + [vmem]...  47.6 us
    ppermute x36, waiting for transfers between devices, swap(): return lax.ppermute(x, axis, [(i, i ^ d) for i in range(n)])  46.2 us
    unnamed x23, local copies, waits for them, and re-layouts  8.18 us
  transfers between devices with their start and end apart: 36, of which 15 were waited for; matrix products, arithmetic and copies ran while one was open for 0% of the time, Pallas kernels for 20%

profile of v2, /device:TPU:2, one launch (start us, length us, event | category | flops | bytes accessed | tf_op | source)
XLA Modules:
  0.0 153.1 jit_solution(15044954754508403974)
XLA Ops:
  4.6 1.6 %project.1 = (f32[192,1024]{1,0:T(8,128)S(1)}, bf16[192,1024]{1,0:T(8,128)(2,1)S(1)}, bf16[192,1024]{1,0:T(8,128)(2,1)S(1)}, bf16[192,1024]{1,0:T(8,128)(2,1)S(1...) custom-call(s32[5]{0:T(128)S(1)} %stack.23.place, ...), custom_call_target="tpu_custom_call" | custom-call | tf_op jit(solution)/shard_map/project/pallas_call | solution.py:56
  6.2 1.7 %collective-permute-start.1 = (bf16[192,1024]{1,0:T(8,128)(2,1)S(1)}, bf16[192,1024]{1,0:T(8,128)(2,1)S(1)}, u32[]{:S(2)}, u32[]{:S(2)}) collective-permute-start(bf16[192,1024]{1,0:T(8,128)(2,1)S(1)} %get-tuple-element.97), channel_id=1, source_target_pairs={{0,1},{1,0},{2,3},{3,2},{4,5},{5,4},{6,7},{7,6},{8,9},{9,8},{10,11... | collective-permute-start | bytes 1179656 | tf_op jit(solution)/shard_map/ppermute | solution.py:499
  7.9 2.2 %collective-permute-start.2 = (bf16[192,1024]{1,0:T(8,128)(2,1)S(1)}, bf16[192,1024]{1,0:T(8,128)(2,1)S(1)}, u32[]{:S(2)}, u32[]{:S(2)}) collective-permute-start(bf16[192,1024]{1,0:T(8,128)(2,1)S(1)} %get-tuple-element.98), channel_id=1, source_target_pairs={{0,3},{1,2},{2,1},{3,0},{4,7},{5,6},{6,5},{7,4},{8,11},{9,10},{10,... | collective-permute-start | bytes 1179656 | tf_op jit(solution)/shard_map/ppermute | solution.py:499
  10.1 2.1 %collective-permute-start = (s32[40,8]{1,0:T(8,128)S(1)}, s32[40,8]{1,0:T(8,128)S(1)}, u32[]{:S(2)}, u32[]{:S(2)}) collective-permute-start(s32[40,8]{1,0:T(8,128)S(1)} %get-tuple-element.96), channel_id=1, source_target_pairs={{0,8},{4,12},{8,0},{12,4},{1,9},{5,13},{9,1},{13,5},{2,10},{6,14},... | collective-permute-start | bytes 3848 | tf_op jit(solution)/shard_map/ppermute | solution.py:499
  12.2 1.4 copy-done.1
  13.6 1.5 leave.1
  15.3 1.8 %collective-permute-done.1.p1 = bf16[192,1024]{1,0:T(8,128)(2,1)S(1)} collective-permute-done((bf16[192,1024]{1,0:T(8,128)(2,1)S(1)}, bf16[192,1024]{1,0:T(8,128)(2,1)S(1)}, u32[]{:S(2)}, u32[]{:S(2)}) %collective-permute-start.1) | collective-permute-done | bytes 393248 | tf_op jit(solution)/shard_map/ppermute | solution.py:499
  17.2 2.5 %collective-permute-done.2.p3 = bf16[192,1024]{1,0:T(8,128)(2,1)S(1)} collective-permute-done((bf16[192,1024]{1,0:T(8,128)(2,1)S(1)}, bf16[192,1024]{1,0:T(8,128)(2,1)S(1)}, u32[]{:S(2)}, u32[]{:S(2)}) %collective-permute-start.2) | collective-permute-done | bytes 393248 | tf_op jit(solution)/shard_map/ppermute | solution.py:499
  19.7 2.1 %collective-permute-start.7 = (bf16[320,1024]{1,0:T(8,128)(2,1)S(1)}, bf16[320,1024]{1,0:T(8,128)(2,1)S(1)}, u32[]{:S(2)}, u32[]{:S(2)}) collective-permute-start(bf16[320,1024]{1,0:T(8,128)(2,1)S(1)} %leave.1), channel_id=1, source_target_pairs={{0,8},{4,12},{8,0},{12,4},{1,9},{5,13},{9,1},{13,5},{2,10},{6,14},... | collective-permute-start | bytes 1966088 | tf_op jit(solution)/shard_map/ppermute | solution.py:499
  21.8 1.7 %collective-permute-start.3 = (bf16[192,1024]{1,0:T(8,128)(2,1)S(1)}, bf16[192,1024]{1,0:T(8,128)(2,1)S(1)}, u32[]{:S(2)}, u32[]{:S(2)}) collective-permute-start(bf16[192,1024]{1,0:T(8,128)(2,1)S(1)} %get-tuple-element.105), channel_id=1, source_target_pairs={{0,2},{1,3},{2,0},{3,1},{4,6},{5,7},{6,4},{7,5},{8,10},{9,11},{10,... | collective-permute-start | bytes 1179656 | tf_op jit(solution)/shard_map/ppermute | solution.py:499
  23.5 2.2 %copy-done.3 = bf16[8,2048,128]{2,1,0:T(8,128)(2,1)S(1)} copy-done((bf16[8,2048,128]{2,1,0:T(8,128)(2,1)S(1)}, bf16[8,2048,128]{2,1,0:T(8,128)(2,1)}, u32[]{:S(2)}) %copy-start.3) | copy-done | bytes 4194328
  25.7 2.8 %embed.1 = (s32[48,8]{1,0:T(8,128)S(1)}, bf16[384,128]{1,0:T(8,128)(2,1)S(1)}, f32[384,1024]{1,0:T(8,128)S(1)}) custom-call(s32[5]{0:T(128)S(1)} %stack.23.place, s32[16,96]{1,0:T(8,128)S(1)} %reshape.23.mask, s32[96,8]{1,0:T(8,128)S(1)} %copy.19.codes, s32[40,8]{1,0:T(8,128)S(1)} %collective-permute-done.codes_come, bf16[8,2048,128]{2,1,0:T(8,128)(2,1)S(1)} %copy-done.3, ...), custom_call_target="tpu_custom_call" | custom-call | tf_op jit(solution)/shard_map/embed/pallas_call | solution.py:56
  28.5 4.2 %collective-permute-done.3.p2 = bf16[192,1024]{1,0:T(8,128)(2,1)S(1)} collective-permute-done((bf16[192,1024]{1,0:T(8,128)(2,1)S(1)}, bf16[192,1024]{1,0:T(8,128)(2,1)S(1)}, u32[]{:S(2)}, u32[]{:S(2)}) %collective-permute-start.3) | collective-permute-done | bytes 393248 | tf_op jit(solution)/shard_map/ppermute | solution.py:499
  33.6 1.5 collective-permute-start.4
  35.1 2.0 %collective-permute-start.6 = (bf16[48,1024]{1,0:T(8,128)(2,1)S(1)}, bf16[48,1024]{1,0:T(8,128)(2,1)S(1)}, u32[]{:S(2)}, u32[]{:S(2)}) collective-permute-start(bf16[48,1024]{1,0:T(8,128)(2,1)S(1)} %get-tuple-element.110), channel_id=1, source_target_pairs={{0,12},{4,8},{8,4},{12,0},{1,13},{5,9},{9,5},{13,1},{2,14},{6,10},... | collective-permute-start | bytes 294920 | tf_op jit(solution)/shard_map/ppermute | solution.py:499
  37.1 1.5 collective-permute-done.7.cot_come
  38.7 1.6 %copy-done.6 = bf16[1024,1024]{1,0:T(8,128)(2,1)S(1)} copy-done((bf16[1024,1024]{1,0:T(8,128)(2,1)S(1)}, bf16[1024,1024]{1,0:T(8,128)(2,1)}, u32[]{:S(2)}) %copy-start.6) | copy-done | bytes 2097176
  40.2 2.7 %upstream.1 = (bf16[384,1024]{1,0:T(8,128)(2,1)S(1)}, f32[384,128]{1,0:T(8,128)S(1)}, bf16[384,1024]{1,0:T(8,128)(2,1)S(1)}, bf16[384,1024]{1,0:T(8,128)(2,1)S(1)}) custom-call(s32[5]{0:T(128)S(1)} %stack.23.place, s32[16,96]{1,0:T(8,128)S(1)} %reshape.23.mask, bf16[768,1024]{1,0:T(8,128)(2,1)S(1)} %bitcast.10, ...), custom_call_target="tpu_custom_call" | custom-call | tf_op jit(solution)/shard_map/upstream/pallas_call | solution.py:56
  43.0 5.9 %forward.1 = (bf16[384,1024]{1,0:T(8,128)(2,1)S(1)}, bf16[384,1024]{1,0:T(8,128)(2,1)S(1)}, bf16[384,3072]{1,0:T(8,128)(2,1)S(1)}, f32[384,1024]{1,0:T(8,128)S(1...) custom-call(f32[48,1024]{1,0:T(8,128)S(1)} %get-tuple-element.107.p0, ...), custom_call_target="tpu_custom_call" | custom-call | tf_op jit(solution)/shard_map/forward/pallas_call | solution.py:56
  49.0 8.3 %backward.1 = (bf16[384,3072]{1,0:T(8,128)(2,1)S(1)}, bf16[4,128,3072]{2,1,0:T(8,128)(2,1)S(1)}) custom-call(s32[5]{0:T(128)S(1)} %stack.23.place, bf16[384,3072]{1,0:T(8,128)(2,1)S(1)} %get-tuple-element.116.packed, f32[3072,256]{1,0:T(8,128)S(1)} %get-tuple-element.117.probs_in, bf16[384,1024]{1,0:T(8,128)(2,1)S(1)} %get-tuple-element.114.grad_mixed, ...), custom_call_target="tpu_custom_call" | custom-call | tf_op jit(solution)/shard_map/backward/pallas_call | solution.py:56
  57.6 6.6 %norm.1 = (bf16[96,1152]{1,0:T(8,128)(2,1)S(1)}, bf16[384,1024]{1,0:T(8,128)(2,1)S(1)}, f32[1024,128]{1,0:T(8,128)S(1)}, bf16[4,128,2176]{2,1,0:T(8,128)(2,1)S(1)}) custom-call(s32[5]{0:T(128)S(1)} %stack.23.place, bf16[384,3072]{1,0:T(8,128)(2,1)S(1)} %get-tuple-element.119.packed_grad, bf16[1024,3072]{1,0:T(8,128)(2,1)S(1)} %bitcast.8, ...), custom_call_target="tpu_custom_call" | custom-call | tf_op jit(solution)/shard_map/norm/pallas_call | solution.py:56
  64.8 2.4 %keep_left.1 = (f32[128,3072]{1,0:T(8,128)S(1)}, bf16[128,3072]{1,0:T(8,128)(2,1)S(1)}, bf16[128,3072]{1,0:T(8,128)(2,1)S(1)}, bf16[128,3072]{1,0:T(8,128)(2,1)S(1)}) custom-call(s32[5]{0:T(128)S(1)} %stack.23.place, bf16[384,1024]{1,0:T(8,128)(2,1)S(1)} %get-tuple-element.118.normed, bf16[384,3072]{1,0:T(8,128)(2,1)S(1)} %get-tuple-element.119.packed_grad, ...), custom_call_target="tpu_custom_call" | custom-call | tf_op jit(solution)/shard_map/keep_left/pallas_call | solution.py:56
  67.2 4.1 %collective-permute-start.15 = (bf16[128,3072]{1,0:T(8,128)(2,1)S(1)}, bf16[128,3072]{1,0:T(8,128)(2,1)S(1)}, u32[]{:S(2)}, u32[]{:S(2)}) collective-permute-start(bf16[128,3072]{1,0:T(8,128)(2,1)S(1)} %get-tuple-element.141), channel_id=1, source_target_pairs={{0,96},{32,64},{64,32},{96,0},{1,97},{33,65},{65,33},{97,1},{2,98}... | collective-permute-start | bytes 2359304 | tf_op jit(solution)/shard_map/ppermute | solution.py:499
  71.4 1.5 collective-permute-start.12
  72.9 1.7 %collective-permute-start.11 = (bf16[96,1152]{1,0:T(8,128)(2,1)S(1)}, bf16[96,1152]{1,0:T(8,128)(2,1)S(1)}, u32[]{:S(2)}, u32[]{:S(2)}) collective-permute-start(bf16[96,1152]{1,0:T(8,128)(2,1)S(1)} %get-tuple-element.127.m0), channel_id=1, source_target_pairs={{0,8},{4,12},{8,0},{12,4},{1,9},{5,13},{9,1},{13,5},{2,10},{6,14},... | collective-permute-start | bytes 663560 | tf_op jit(solution)/shard_map/ppermute | solution.py:499
  75.5 2.2 %keep_right.1 = (f32[4,32,2176]{2,1,0:T(8,128)S(1)}, bf16[4,32,2176]{2,1,0:T(8,128)(2,1)S(1)}, bf16[4,32,2176]{2,1,0:T(8,128)(2,1)S(1)}, bf16[4,32,2176]{2,1,0:T(8,128)(2,1)S(1)}) custom-call(s32[5]{0:T(128)S(1)} %stack.23.place, bf16[384,1024]{1,0:T(8,128)(2,1)S(1)} %get-tuple-element.125.mixed, bf16[384,1024]{1,0:T(8,128)(2,1)S(1)} %get-tuple-element.126.grad_low, ...), custom_call_target="tpu_custom_call" | custom-call | tf_op jit(solution)/shard_map/keep_right/pallas_call | solution.py:56
  77.7 5.5 %collective-permute-done.12.m3 = bf16[96,1152]{1,0:T(8,128)(2,1)S(1)} collective-permute-done((bf16[96,1152]{1,0:T(8,128)(2,1)S(1)}, bf16[96,1152]{1,0:T(8,128)(2,1)S(1)}, u32[]{:S(2)}, u32[]{:S(2)}) %collective-permute-start.12) | collective-permute-done | bytes 221216 | tf_op jit(solution)/shard_map/ppermute | solution.py:499
  83.2 1.5 collective-permute-start.17
  84.7 2.8 %collective-permute-start.16 = (bf16[4,32,2176]{2,1,0:T(8,128)(2,1)S(1)}, bf16[4,32,2176]{2,1,0:T(8,128)(2,1)S(1)}, u32[]{:S(2)}, u32[]{:S(2)}) collective-permute-start(bf16[4,32,2176]{2,1,0:T(8,128)(2,1)S(1)} %get-tuple-element.138), channel_id=1, source_target_pairs={{0,4},{4,0},{8,12},{12,8},{1,5},{5,1},{9,13},{13,9},{2,6},{6,2},{1... | collective-permute-start | bytes 1671176 | tf_op jit(solution)/shard_map/ppermute | solution.py:499
  87.5 3.7 %table.3 = (bf16[4,32,2048]{2,1,0:T(8,128)(2,1)S(1)}, f32[4,32,2048]{2,1,0:T(8,128)S(1)}) custom-call(s32[5]{0:T(128)S(1)} %stack.23.place, bf16[96,1152]{1,0:T(8,128)(2,1)S(1)} %get-tuple-element.127.m0, bf16[96,1152]{1,0:T(8,128)(2,1)S(1)} %collective-permute-done.10.m1, bf16[96,1152]{1,0:T(8,128)(2,1)S(1)} %collective-permute-done.11.m2, ...), custom_call_target="tpu_custom_call" | custom-call | tf_op jit(solution)/shard_map/table/pallas_call | solution.py:56
  91.4 1.8 %collective-permute-done.13.got = bf16[4,32,2048]{2,1,0:T(8,128)(2,1)S(1)} collective-permute-done((bf16[4,32,2048]{2,1,0:T(8,128)(2,1)S(1)}, bf16[4,32,2048]{2,1,0:T(8,128)(2,1)S(1)}, u32[]{:S(2)}, u32[]{:S(2)}) %collective-permute-start.13) | collective-permute-done | bytes 524320 | tf_op jit(solution)/shard_map/ppermute | solution.py:499
  93.2 3.2 %collective-permute-done.17.g3 = bf16[4,32,2176]{2,1,0:T(8,128)(2,1)S(1)} collective-permute-done((bf16[4,32,2176]{2,1,0:T(8,128)(2,1)S(1)}, bf16[4,32,2176]{2,1,0:T(8,128)(2,1)S(1)}, u32[]{:S(2)}, u32[]{:S(2)}) %collective-permute-start.17) | collective-permute-done | bytes 557088 | tf_op jit(solution)/shard_map/ppermute | solution.py:499
  96.4 2.5 %collective-permute-done.16.g1 = bf16[4,32,2176]{2,1,0:T(8,128)(2,1)S(1)} collective-permute-done((bf16[4,32,2176]{2,1,0:T(8,128)(2,1)S(1)}, bf16[4,32,2176]{2,1,0:T(8,128)(2,1)S(1)}, u32[]{:S(2)}, u32[]{:S(2)}) %collective-permute-start.16) | collective-permute-done | bytes 557088 | tf_op jit(solution)/shard_map/ppermute | solution.py:499
  98.9 1.6 %collective-permute-start.18 = (bf16[128,3072]{1,0:T(8,128)(2,1)S(1)}, bf16[128,3072]{1,0:T(8,128)(2,1)S(1)}, u32[]{:S(2)}, u32[]{:S(2)}) collective-permute-start(bf16[128,3072]{1,0:T(8,128)(2,1)S(1)} %get-tuple-element.144), channel_id=1, source_target_pairs={{0,64},{32,96},{64,0},{96,32},{1,65},{33,97},{65,1},{97,33},{2,66}... | collective-permute-start | bytes 2359304 | tf_op jit(solution)/shard_map/ppermute | solution.py:499
  100.4 2.1 %collective-permute-start.22 = (bf16[4,32,2176]{2,1,0:T(8,128)(2,1)S(1)}, bf16[4,32,2176]{2,1,0:T(8,128)(2,1)S(1)}, u32[]{:S(2)}, u32[]{:S(2)}) collective-permute-start(bf16[4,32,2176]{2,1,0:T(8,128)(2,1)S(1)} %get-tuple-element.152), channel_id=1, source_target_pairs={{0,8},{4,12},{8,0},{12,4},{1,9},{5,13},{9,1},{13,5},{2,10},{6,14},... | collective-permute-start | bytes 1671176 | tf_op jit(solution)/shard_map/ppermute | solution.py:499
  102.6 2.2 %collective-permute-start.28 = (bf16[192,1024]{1,0:T(8,128)(2,1)S(1)}, bf16[192,1024]{1,0:T(8,128)(2,1)S(1)}, u32[]{:S(2)}, u32[]{:S(2)}) collective-permute-start(bf16[192,1024]{1,0:T(8,128)(2,1)S(1)} %pad_maximum_fusion.p0), channel_id=1, source_target_pairs={{0,3},{1,2},{2,1},{3,0},{4,7},{5,6},{6,5},{7,4},{8,11},{9,10},{10,... | collective-permute-start | bytes 1179656 | tf_op jit(solution)/shard_map/ppermute | solution.py:499
  104.8 1.9 %collective-permute-start.26 = (bf16[192,1024]{1,0:T(8,128)(2,1)S(1)}, bf16[192,1024]{1,0:T(8,128)(2,1)S(1)}, u32[]{:S(2)}, u32[]{:S(2)}) collective-permute-start(bf16[192,1024]{1,0:T(8,128)(2,1)S(1)} %pad_maximum_fusion.p0), channel_id=1, source_target_pairs={{0,1},{1,0},{2,3},{3,2},{4,5},{5,4},{6,7},{7,6},{8,9},{9,8},{10,11... | collective-permute-start | bytes 1179656 | tf_op jit(solution)/shard_map/ppermute | solution.py:499
  106.7 7.5 %collective-permute-done.22.g2 = bf16[4,32,2176]{2,1,0:T(8,128)(2,1)S(1)} collective-permute-done((bf16[4,32,2176]{2,1,0:T(8,128)(2,1)S(1)}, bf16[4,32,2176]{2,1,0:T(8,128)(2,1)S(1)}, u32[]{:S(2)}, u32[]{:S(2)}) %collective-permute-start.22) | collective-permute-done | bytes 557088 | tf_op jit(solution)/shard_map/ppermute | solution.py:499
  115.2 5.4 %collective-permute-done.28.p3 = bf16[192,1024]{1,0:T(8,128)(2,1)S(1)} collective-permute-done((bf16[192,1024]{1,0:T(8,128)(2,1)S(1)}, bf16[192,1024]{1,0:T(8,128)(2,1)S(1)}, u32[]{:S(2)}, u32[]{:S(2)}) %collective-permute-start.28) | collective-permute-done | bytes 393248 | tf_op jit(solution)/shard_map/ppermute | solution.py:499
  121.2 1.7 %win.1 = (bf16[4,256,128]{2,1,0:T(8,128)(2,1)S(1)}, f32[4,256,128]{2,1,0:T(8,128)S(1)}) custom-call(s32[5]{0:T(128)S(1)} %stack.23.place, bf16[192,1024]{1,0:T(8,128)(2,1)S(1)} %pad_maximum_fusion.p0, bf16[192,1024]{1,0:T(8,128)(2,1)S(1)} %collective-permute-done.26.p1, bf16[192,1024]{1,0:T(8,128)(2,1)S(1)} %collective-permute-done.27.p2, ...), custom_call_target="tpu_custom_call" | custom-call | tf_op jit(solution)/shard_map/win/pallas_call | solution.py:56
  123.1 2.1 %collective-permute-start.24 = (bf16[32,4224]{1,0:T(8,128)(2,1)S(1)}, bf16[32,4224]{1,0:T(8,128)(2,1)S(1)}, u32[]{:S(2)}, u32[]{:S(2)}) collective-permute-start(bf16[32,4224]{1,0:T(8,128)(2,1)S(1)} %get-tuple-element.158), channel_id=1, source_target_pairs={{0,64},{32,96},{64,0},{96,32},{1,65},{33,97},{65,1},{97,33},{2,66}... | collective-permute-start | bytes 811016 | tf_op jit(solution)/shard_map/ppermute | solution.py:499
  127.2 2.2 %collective-permute-start.20 = (bf16[32,3072]{1,0:T(8,128)(2,1)S(1)}, bf16[32,3072]{1,0:T(8,128)(2,1)S(1)}, u32[]{:S(2)}, u32[]{:S(2)}) collective-permute-start(bf16[32,3072]{1,0:T(8,128)(2,1)S(1)} %get-tuple-element.148), channel_id=1, source_target_pairs={{0,8},{4,12},{8,0},{12,4},{1,9},{5,13},{9,1},{13,5},{2,10},{6,14},... | collective-permute-start | bytes 589832 | tf_op jit(solution)/shard_map/ppermute | solution.py:499
  131.3 2.3 %collective-permute-done.24.r2 = bf16[32,4224]{1,0:T(8,128)(2,1)S(1)} collective-permute-done((bf16[32,4224]{1,0:T(8,128)(2,1)S(1)}, bf16[32,4224]{1,0:T(8,128)(2,1)S(1)}, u32[]{:S(2)}, u32[]{:S(2)}) %collective-permute-start.24) | collective-permute-done | bytes 270368 | tf_op jit(solution)/shard_map/ppermute | solution.py:499
  133.7 5.6 %collective-permute-done.25.r3 = bf16[32,4224]{1,0:T(8,128)(2,1)S(1)} collective-permute-done((bf16[32,4224]{1,0:T(8,128)(2,1)S(1)}, bf16[32,4224]{1,0:T(8,128)(2,1)S(1)}, u32[]{:S(2)}, u32[]{:S(2)}) %collective-permute-start.25) | collective-permute-done | bytes 270368 | tf_op jit(solution)/shard_map/ppermute | solution.py:499
  139.3 1.8 %collective-permute-start.31 = (bf16[256,128]{1,0:T(8,128)(2,1)S(1)}, bf16[256,128]{1,0:T(8,128)(2,1)S(1)}, u32[]{:S(2)}, u32[]{:S(2)}) collective-permute-start(bf16[256,128]{1,0:T(8,128)(2,1)S(1)} %get-tuple-element.169), channel_id=1, source_target_pairs={{0,64},{32,96},{64,0},{96,32},{1,65},{33,97},{65,1},{97,33},{2,66}... | collective-permute-start | bytes 196616 | tf_op jit(solution)/shard_map/ppermute | solution.py:499
  143.0 1.8 %collective-permute-start.34 = (bf16[16,3712]{1,0:T(8,128)(2,1)S(1)}, bf16[16,3712]{1,0:T(8,128)(2,1)S(1)}, u32[]{:S(2)}, u32[]{:S(2)}) collective-permute-start(bf16[16,3712]{1,0:T(8,128)(2,1)S(1)} %get-tuple-element.172), channel_id=1, source_target_pairs={{0,2},{1,3},{2,0},{3,1},{4,6},{5,7},{6,4},{7,5},{8,10},{9,11},{10,... | collective-permute-start | bytes 356360 | tf_op jit(solution)/shard_map/ppermute | solution.py:499
  147.3 2.8 %temporal.3 = bf16[1536,256]{1,0:T(8,128)(2,1)} custom-call(s32[5]{0:T(128)S(1)} %stack.23.place, s32[16,96]{1,0:T(8,128)S(1)} %get-tuple-element.162.keeps, s32[16,96]{1,0:T(8,128)S(1)} %get-tuple-element.163.goes, bf16[192,1024]{1,0:T(8,128)(2,1)S(1)} %pad_maximum_fusion.p0, bf16[192,1024]{1,0:T(8,128)(2,1)S(1)} %collective-permute-done.26.p1, ...), custom_call_target="tpu_custom_call" | custom-call | tf_op jit(solution)/shard_map/temporal/pallas_call | solution.py:56
  150.1 1.6 %collective-permute-done.35.d = bf16[16,3712]{1,0:T(8,128)(2,1)S(1)} collective-permute-done((bf16[16,3712]{1,0:T(8,128)(2,1)S(1)}, bf16[16,3712]{1,0:T(8,128)(2,1)S(1)}, u32[]{:S(2)}, u32[]{:S(2)}) %collective-permute-start.35) | collective-permute-done | bytes 118816 | tf_op jit(solution)/shard_map/ppermute | solution.py:499
  (75 shorter events, 18.7 us)
Async XLA Ops:
  0.6 22.9 %copy-start = (bf16[8,128,1024]{2,1,0:T(8,128)(2,1)S(1)}, bf16[8,128,1024]{2,1,0:T(8,128)(2,1)}, u32[]{:S(2)}) copy-start(bf16[8,128,1024]{2,1,0:T(8,128)(2,1)} %adapter_b.3) | copy-start | bytes 6291460
  2.4 1.0 copy-start.4
  3.5 1.1 copy-start.7
  6.2 10.9 %collective-permute-start.1 = (bf16[192,1024]{1,0:T(8,128)(2,1)S(1)}, bf16[192,1024]{1,0:T(8,128)(2,1)S(1)}, u32[]{:S(2)}, u32[]{:S(2)}) collective-permute-start(bf16[192,1024]{1,0:T(8,128)(2,1)S(1)} %get-tuple-element.97), channel_id=1, source_target_pairs={{0,1},{1,0},{2,3},{3,2},{4,5},{5,4},{6,7},{7,6},{8,9},{9,8},{10,11... | collective-permute-start | bytes 1179656 | tf_op jit(solution)/shard_map/ppermute | solution.py:499
  7.9 11.8 %collective-permute-start.2 = (bf16[192,1024]{1,0:T(8,128)(2,1)S(1)}, bf16[192,1024]{1,0:T(8,128)(2,1)S(1)}, u32[]{:S(2)}, u32[]{:S(2)}) collective-permute-start(bf16[192,1024]{1,0:T(8,128)(2,1)S(1)} %get-tuple-element.98), channel_id=1, source_target_pairs={{0,3},{1,2},{2,1},{3,0},{4,7},{5,6},{6,5},{7,4},{8,11},{9,10},{10,... | collective-permute-start | bytes 1179656 | tf_op jit(solution)/shard_map/ppermute | solution.py:499
  10.1 5.3 %collective-permute-start = (s32[40,8]{1,0:T(8,128)S(1)}, s32[40,8]{1,0:T(8,128)S(1)}, u32[]{:S(2)}, u32[]{:S(2)}) collective-permute-start(s32[40,8]{1,0:T(8,128)S(1)} %get-tuple-element.96), channel_id=1, source_target_pairs={{0,8},{4,12},{8,0},{12,4},{1,9},{5,13},{9,1},{13,5},{2,10},{6,14},... | collective-permute-start | bytes 3848 | tf_op jit(solution)/shard_map/ppermute | solution.py:499
  12.2 1.4 copy-start.1
  19.7 23.3 %slice-start = ((s8[6291456]{0:T(1024)(128)(4,1)}), s8[4194304]{0:T(1024)(128)(4,1)S(1)}, s32[]{:S(2)}) async-start(s8[6291456]{0:T(1024)(128)(4,1)} %bitcast.7), calls=%async_computation | async-start | bytes 8388608
  19.7 23.3 %slice-start.1 = ((s8[6291456]{0:T(1024)(128)(4,1)}), s8[2097152]{0:T(1024)(128)(4,1)S(1)}, s32[]{:S(2)}) async-start(s8[6291456]{0:T(1024)(128)(4,1)} %bitcast.7), calls=%async_computation.1 | async-start | bytes 4194304
  19.7 19.0 %collective-permute-start.7 = (bf16[320,1024]{1,0:T(8,128)(2,1)S(1)}, bf16[320,1024]{1,0:T(8,128)(2,1)S(1)}, u32[]{:S(2)}, u32[]{:S(2)}) collective-permute-start(bf16[320,1024]{1,0:T(8,128)(2,1)S(1)} %leave.1), channel_id=1, source_target_pairs={{0,8},{4,12},{8,0},{12,4},{1,9},{5,13},{9,1},{13,5},{2,10},{6,14},... | collective-permute-start | bytes 1966088 | tf_op jit(solution)/shard_map/ppermute | solution.py:499
  21.8 10.9 %collective-permute-start.3 = (bf16[192,1024]{1,0:T(8,128)(2,1)S(1)}, bf16[192,1024]{1,0:T(8,128)(2,1)S(1)}, u32[]{:S(2)}, u32[]{:S(2)}) collective-permute-start(bf16[192,1024]{1,0:T(8,128)(2,1)S(1)} %get-tuple-element.105), channel_id=1, source_target_pairs={{0,2},{1,3},{2,0},{3,1},{4,6},{5,7},{6,4},{7,5},{8,10},{9,11},{10,... | collective-permute-start | bytes 1179656 | tf_op jit(solution)/shard_map/ppermute | solution.py:499
  23.5 2.2 %copy-start.3 = (bf16[8,2048,128]{2,1,0:T(8,128)(2,1)S(1)}, bf16[8,2048,128]{2,1,0:T(8,128)(2,1)}, u32[]{:S(2)}) copy-start(bf16[8,2048,128]{2,1,0:T(8,128)(2,1)} %table.2) | copy-start | bytes 12582916
  28.5 10.1 %copy-start.2 = (bf16[96,8,1024]{2,1,0:T(8,128)(2,1)S(1)}, bf16[96,8,1024]{2,1,0:T(8,128)(2,1)}, u32[]{:S(2)}) copy-start(bf16[96,8,1024]{2,1,0:T(8,128)(2,1)} %param.15) | copy-start | bytes 4718596
  33.5 9.5 %copy-start.8 = (f32[1024]{0:T(1024)S(1)}, f32[1024]{0:T(1024)}, u32[]{:S(2)}) copy-start(f32[1024]{0:T(1024)} %param.16) | copy-start | bytes 12292
  33.6 9.4 %collective-permute-start.4 = (bf16[48,1024]{1,0:T(8,128)(2,1)S(1)}, bf16[48,1024]{1,0:T(8,128)(2,1)S(1)}, u32[]{:S(2)}, u32[]{:S(2)}) collective-permute-start(bf16[48,1024]{1,0:T(8,128)(2,1)S(1)} %get-tuple-element.108), channel_id=1, source_target_pairs={{0,4},{4,0},{8,12},{12,8},{1,5},{5,1},{9,13},{13,9},{2,6},{6,2},{1... | collective-permute-start | bytes 294920 | tf_op jit(solution)/shard_map/ppermute | solution.py:499
  35.1 7.9 %collective-permute-start.5 = (bf16[48,1024]{1,0:T(8,128)(2,1)S(1)}, bf16[48,1024]{1,0:T(8,128)(2,1)S(1)}, u32[]{:S(2)}, u32[]{:S(2)}) collective-permute-start(bf16[48,1024]{1,0:T(8,128)(2,1)S(1)} %get-tuple-element.109), channel_id=1, source_target_pairs={{0,8},{4,12},{8,0},{12,4},{1,9},{5,13},{9,1},{13,5},{2,10},{6,14},... | collective-permute-start | bytes 294920 | tf_op jit(solution)/shard_map/ppermute | solution.py:499
  35.1 7.9 %collective-permute-start.6 = (bf16[48,1024]{1,0:T(8,128)(2,1)S(1)}, bf16[48,1024]{1,0:T(8,128)(2,1)S(1)}, u32[]{:S(2)}, u32[]{:S(2)}) collective-permute-start(bf16[48,1024]{1,0:T(8,128)(2,1)S(1)} %get-tuple-element.110), channel_id=1, source_target_pairs={{0,12},{4,8},{8,4},{12,0},{1,13},{5,9},{9,5},{13,1},{2,14},{6,10},... | collective-permute-start | bytes 294920 | tf_op jit(solution)/shard_map/ppermute | solution.py:499
  38.7 1.6 %copy-start.6 = (bf16[1024,1024]{1,0:T(8,128)(2,1)S(1)}, bf16[1024,1024]{1,0:T(8,128)(2,1)}, u32[]{:S(2)}) copy-start(bf16[1024,1024]{1,0:T(8,128)(2,1)} %w_out.1) | copy-start | bytes 6291460
  57.3 7.5 %collective-permute-start.8 = (bf16[4,128,3072]{2,1,0:T(8,128)(2,1)S(1)}, bf16[4,128,3072]{2,1,0:T(8,128)(2,1)S(1)}, u32[]{:S(2)}, u32[]{:S(2)}) collective-permute-start(bf16[4,128,3072]{2,1,0:T(8,128)(2,1)S(1)} %get-tuple-element.129), channel_id=1, source_target_pairs={{0,16},{16,0},{1,17},{17,1},{2,18},{18,2},{3,19},{19,3},{4,20},{20... | collective-permute-start | bytes 9437192 | tf_op jit(solution)/shard_map/ppermute | solution.py:499
  64.3 10.3 %collective-permute-start.9 = (bf16[4,128,2176]{2,1,0:T(8,128)(2,1)S(1)}, bf16[4,128,2176]{2,1,0:T(8,128)(2,1)S(1)}, u32[]{:S(2)}, u32[]{:S(2)}) collective-permute-start(bf16[4,128,2176]{2,1,0:T(8,128)(2,1)S(1)} %get-tuple-element.136), channel_id=1, source_target_pairs={{0,16},{16,0},{1,17},{17,1},{2,18},{18,2},{3,19},{19,3},{4,20},{20... | collective-permute-start | bytes 6684680 | tf_op jit(solution)/shard_map/ppermute | solution.py:499
  67.2 31.6 %collective-permute-start.15 = (bf16[128,3072]{1,0:T(8,128)(2,1)S(1)}, bf16[128,3072]{1,0:T(8,128)(2,1)S(1)}, u32[]{:S(2)}, u32[]{:S(2)}) collective-permute-start(bf16[128,3072]{1,0:T(8,128)(2,1)S(1)} %get-tuple-element.141), channel_id=1, source_target_pairs={{0,96},{32,64},{64,32},{96,0},{1,97},{33,65},{65,33},{97,1},{2,98}... | collective-permute-start | bytes 2359304 | tf_op jit(solution)/shard_map/ppermute | solution.py:499
  71.4 27.5 %collective-permute-start.14 = (bf16[128,3072]{1,0:T(8,128)(2,1)S(1)}, bf16[128,3072]{1,0:T(8,128)(2,1)S(1)}, u32[]{:S(2)}, u32[]{:S(2)}) collective-permute-start(bf16[128,3072]{1,0:T(8,128)(2,1)S(1)} %get-tuple-element.132), channel_id=1, source_target_pairs={{0,32},{32,0},{64,96},{96,64},{1,33},{33,1},{65,97},{97,65},{2,34}... | collective-permute-start | bytes 2359304 | tf_op jit(solution)/shard_map/ppermute | solution.py:499
  71.4 11.8 %collective-permute-start.12 = (bf16[96,1152]{1,0:T(8,128)(2,1)S(1)}, bf16[96,1152]{1,0:T(8,128)(2,1)S(1)}, u32[]{:S(2)}, u32[]{:S(2)}) collective-permute-start(bf16[96,1152]{1,0:T(8,128)(2,1)S(1)} %get-tuple-element.127.m0), channel_id=1, source_target_pairs={{0,12},{4,8},{8,4},{12,0},{1,13},{5,9},{9,5},{13,1},{2,14},{6,10},... | collective-permute-start | bytes 663560 | tf_op jit(solution)/shard_map/ppermute | solution.py:499
  72.9 11.8 %collective-permute-start.11 = (bf16[96,1152]{1,0:T(8,128)(2,1)S(1)}, bf16[96,1152]{1,0:T(8,128)(2,1)S(1)}, u32[]{:S(2)}, u32[]{:S(2)}) collective-permute-start(bf16[96,1152]{1,0:T(8,128)(2,1)S(1)} %get-tuple-element.127.m0), channel_id=1, source_target_pairs={{0,8},{4,12},{8,0},{12,4},{1,9},{5,13},{9,1},{13,5},{2,10},{6,14},... | collective-permute-start | bytes 663560 | tf_op jit(solution)/shard_map/ppermute | solution.py:499
  74.6 12.9 %collective-permute-start.10 = (bf16[96,1152]{1,0:T(8,128)(2,1)S(1)}, bf16[96,1152]{1,0:T(8,128)(2,1)S(1)}, u32[]{:S(2)}, u32[]{:S(2)}) collective-permute-start(bf16[96,1152]{1,0:T(8,128)(2,1)S(1)} %get-tuple-element.127.m0), channel_id=1, source_target_pairs={{0,4},{4,0},{8,12},{12,8},{1,5},{5,1},{9,13},{13,9},{2,6},{6,2},{1... | collective-permute-start | bytes 663560 | tf_op jit(solution)/shard_map/ppermute | solution.py:499
  83.2 13.2 %collective-permute-start.17 = (bf16[4,32,2176]{2,1,0:T(8,128)(2,1)S(1)}, bf16[4,32,2176]{2,1,0:T(8,128)(2,1)S(1)}, u32[]{:S(2)}, u32[]{:S(2)}) collective-permute-start(bf16[4,32,2176]{2,1,0:T(8,128)(2,1)S(1)} %get-tuple-element.142), channel_id=1, source_target_pairs={{0,12},{4,8},{8,4},{12,0},{1,13},{5,9},{9,5},{13,1},{2,14},{6,10},... | collective-permute-start | bytes 1671176 | tf_op jit(solution)/shard_map/ppermute | solution.py:499
  84.7 14.2 %collective-permute-start.16 = (bf16[4,32,2176]{2,1,0:T(8,128)(2,1)S(1)}, bf16[4,32,2176]{2,1,0:T(8,128)(2,1)S(1)}, u32[]{:S(2)}, u32[]{:S(2)}) collective-permute-start(bf16[4,32,2176]{2,1,0:T(8,128)(2,1)S(1)} %get-tuple-element.138), channel_id=1, source_target_pairs={{0,4},{4,0},{8,12},{12,8},{1,5},{5,1},{9,13},{13,9},{2,6},{6,2},{1... | collective-permute-start | bytes 1671176 | tf_op jit(solution)/shard_map/ppermute | solution.py:499
  91.2 2.0 %collective-permute-start.13 = (bf16[4,32,2048]{2,1,0:T(8,128)(2,1)S(1)}, bf16[4,32,2048]{2,1,0:T(8,128)(2,1)S(1)}, u32[]{:S(2)}, u32[]{:S(2)}) collective-permute-start(bf16[4,32,2048]{2,1,0:T(8,128)(2,1)S(1)} %get-tuple-element.140), channel_id=1, source_target_pairs={{0,16},{16,0},{1,17},{17,1},{2,18},{18,2},{3,19},{19,3},{4,20},{20... | collective-permute-start | bytes 1572872 | tf_op jit(solution)/shard_map/ppermute | solution.py:499
  98.9 27.1 %collective-permute-start.18 = (bf16[128,3072]{1,0:T(8,128)(2,1)S(1)}, bf16[128,3072]{1,0:T(8,128)(2,1)S(1)}, u32[]{:S(2)}, u32[]{:S(2)}) collective-permute-start(bf16[128,3072]{1,0:T(8,128)(2,1)S(1)} %get-tuple-element.144), channel_id=1, source_target_pairs={{0,64},{32,96},{64,0},{96,32},{1,65},{33,97},{65,1},{97,33},{2,66}... | collective-permute-start | bytes 2359304 | tf_op jit(solution)/shard_map/ppermute | solution.py:499
  100.4 13.7 %collective-permute-start.22 = (bf16[4,32,2176]{2,1,0:T(8,128)(2,1)S(1)}, bf16[4,32,2176]{2,1,0:T(8,128)(2,1)S(1)}, u32[]{:S(2)}, u32[]{:S(2)}) collective-permute-start(bf16[4,32,2176]{2,1,0:T(8,128)(2,1)S(1)} %get-tuple-element.152), channel_id=1, source_target_pairs={{0,8},{4,12},{8,0},{12,4},{1,9},{5,13},{9,1},{13,5},{2,10},{6,14},... | collective-permute-start | bytes 1671176 | tf_op jit(solution)/shard_map/ppermute | solution.py:499
  102.6 18.0 %collective-permute-start.28 = (bf16[192,1024]{1,0:T(8,128)(2,1)S(1)}, bf16[192,1024]{1,0:T(8,128)(2,1)S(1)}, u32[]{:S(2)}, u32[]{:S(2)}) collective-permute-start(bf16[192,1024]{1,0:T(8,128)(2,1)S(1)} %pad_maximum_fusion.p0), channel_id=1, source_target_pairs={{0,3},{1,2},{2,1},{3,0},{4,7},{5,6},{6,5},{7,4},{8,11},{9,10},{10,... | collective-permute-start | bytes 1179656 | tf_op jit(solution)/shard_map/ppermute | solution.py:499
  104.7 15.9 %collective-permute-start.27 = (bf16[192,1024]{1,0:T(8,128)(2,1)S(1)}, bf16[192,1024]{1,0:T(8,128)(2,1)S(1)}, u32[]{:S(2)}, u32[]{:S(2)}) collective-permute-start(bf16[192,1024]{1,0:T(8,128)(2,1)S(1)} %pad_maximum_fusion.p0), channel_id=1, source_target_pairs={{0,2},{1,3},{2,0},{3,1},{4,6},{5,7},{6,4},{7,5},{8,10},{9,11},{10,... | collective-permute-start | bytes 1179656 | tf_op jit(solution)/shard_map/ppermute | solution.py:499
  104.8 16.5 %collective-permute-start.26 = (bf16[192,1024]{1,0:T(8,128)(2,1)S(1)}, bf16[192,1024]{1,0:T(8,128)(2,1)S(1)}, u32[]{:S(2)}, u32[]{:S(2)}) collective-permute-start(bf16[192,1024]{1,0:T(8,128)(2,1)S(1)} %pad_maximum_fusion.p0), channel_id=1, source_target_pairs={{0,1},{1,0},{2,3},{3,2},{4,5},{5,4},{6,7},{7,6},{8,9},{9,8},{10,11... | collective-permute-start | bytes 1179656 | tf_op jit(solution)/shard_map/ppermute | solution.py:499
  115.0 14.4 %collective-permute-start.23 = (bf16[32,4224]{1,0:T(8,128)(2,1)S(1)}, bf16[32,4224]{1,0:T(8,128)(2,1)S(1)}, u32[]{:S(2)}, u32[]{:S(2)}) collective-permute-start(bf16[32,4224]{1,0:T(8,128)(2,1)S(1)} %get-tuple-element.157), channel_id=1, source_target_pairs={{0,32},{32,0},{64,96},{96,64},{1,33},{33,1},{65,97},{97,65},{2,34}... | collective-permute-start | bytes 811016 | tf_op jit(solution)/shard_map/ppermute | solution.py:499
  123.0 4.3 %collective-permute-start.29 = (bf16[4,256,128]{2,1,0:T(8,128)(2,1)S(1)}, bf16[4,256,128]{2,1,0:T(8,128)(2,1)S(1)}, u32[]{:S(2)}, u32[]{:S(2)}) collective-permute-start(bf16[4,256,128]{2,1,0:T(8,128)(2,1)S(1)} %get-tuple-element.166), channel_id=1, source_target_pairs={{0,16},{16,0},{1,17},{17,1},{2,18},{18,2},{3,19},{19,3},{4,20},{20... | collective-permute-start | bytes 786440 | tf_op jit(solution)/shard_map/ppermute | solution.py:499
  123.1 10.5 %collective-permute-start.24 = (bf16[32,4224]{1,0:T(8,128)(2,1)S(1)}, bf16[32,4224]{1,0:T(8,128)(2,1)S(1)}, u32[]{:S(2)}, u32[]{:S(2)}) collective-permute-start(bf16[32,4224]{1,0:T(8,128)(2,1)S(1)} %get-tuple-element.158), channel_id=1, source_target_pairs={{0,64},{32,96},{64,0},{96,32},{1,65},{33,97},{65,1},{97,33},{2,66}... | collective-permute-start | bytes 811016 | tf_op jit(solution)/shard_map/ppermute | solution.py:499
  125.1 14.1 %collective-permute-start.25 = (bf16[32,4224]{1,0:T(8,128)(2,1)S(1)}, bf16[32,4224]{1,0:T(8,128)(2,1)S(1)}, u32[]{:S(2)}, u32[]{:S(2)}) collective-permute-start(bf16[32,4224]{1,0:T(8,128)(2,1)S(1)} %get-tuple-element.159), channel_id=1, source_target_pairs={{0,96},{32,64},{64,32},{96,0},{1,97},{33,65},{65,33},{97,1},{2,98}... | collective-permute-start | bytes 811016 | tf_op jit(solution)/shard_map/ppermute | solution.py:499
  127.1 20.1 %copy-start.5 = (bf16[256,1024]{1,0:T(8,128)(2,1)S(1)}, bf16[256,1024]{1,0:T(8,128)(2,1)}, u32[]{:S(2)}) copy-start(bf16[256,1024]{1,0:T(8,128)(2,1)} %w_in.3) | copy-start | bytes 1572868
  127.1 13.9 %collective-permute-start.19 = (bf16[32,3072]{1,0:T(8,128)(2,1)S(1)}, bf16[32,3072]{1,0:T(8,128)(2,1)S(1)}, u32[]{:S(2)}, u32[]{:S(2)}) collective-permute-start(bf16[32,3072]{1,0:T(8,128)(2,1)S(1)} %get-tuple-element.147), channel_id=1, source_target_pairs={{0,4},{4,0},{8,12},{12,8},{1,5},{5,1},{9,13},{13,9},{2,6},{6,2},{1... | collective-permute-start | bytes 589832 | tf_op jit(solution)/shard_map/ppermute | solution.py:499
  127.2 14.8 %collective-permute-start.20 = (bf16[32,3072]{1,0:T(8,128)(2,1)S(1)}, bf16[32,3072]{1,0:T(8,128)(2,1)S(1)}, u32[]{:S(2)}, u32[]{:S(2)}) collective-permute-start(bf16[32,3072]{1,0:T(8,128)(2,1)S(1)} %get-tuple-element.148), channel_id=1, source_target_pairs={{0,8},{4,12},{8,0},{12,4},{1,9},{5,13},{9,1},{13,5},{2,10},{6,14},... | collective-permute-start | bytes 589832 | tf_op jit(solution)/shard_map/ppermute | solution.py:499
  129.5 12.6 %collective-permute-start.21 = (bf16[32,3072]{1,0:T(8,128)(2,1)S(1)}, bf16[32,3072]{1,0:T(8,128)(2,1)S(1)}, u32[]{:S(2)}, u32[]{:S(2)}) collective-permute-start(bf16[32,3072]{1,0:T(8,128)(2,1)S(1)} %get-tuple-element.149), channel_id=1, source_target_pairs={{0,12},{4,8},{8,4},{12,0},{1,13},{5,9},{9,5},{13,1},{2,14},{6,10},... | collective-permute-start | bytes 589832 | tf_op jit(solution)/shard_map/ppermute | solution.py:499
  133.6 12.5 %collective-permute-start.30 = (bf16[256,128]{1,0:T(8,128)(2,1)S(1)}, bf16[256,128]{1,0:T(8,128)(2,1)S(1)}, u32[]{:S(2)}, u32[]{:S(2)}) collective-permute-start(bf16[256,128]{1,0:T(8,128)(2,1)S(1)} %get-tuple-element.168), channel_id=1, source_target_pairs={{0,32},{32,0},{64,96},{96,64},{1,33},{33,1},{65,97},{97,65},{2,34}... | collective-permute-start | bytes 196616 | tf_op jit(solution)/shard_map/ppermute | solution.py:499
  139.3 7.3 %collective-permute-start.31 = (bf16[256,128]{1,0:T(8,128)(2,1)S(1)}, bf16[256,128]{1,0:T(8,128)(2,1)S(1)}, u32[]{:S(2)}, u32[]{:S(2)}) collective-permute-start(bf16[256,128]{1,0:T(8,128)(2,1)S(1)} %get-tuple-element.169), channel_id=1, source_target_pairs={{0,64},{32,96},{64,0},{96,32},{1,65},{33,97},{65,1},{97,33},{2,66}... | collective-permute-start | bytes 196616 | tf_op jit(solution)/shard_map/ppermute | solution.py:499
  141.1 5.5 %collective-permute-start.32 = (bf16[256,128]{1,0:T(8,128)(2,1)S(1)}, bf16[256,128]{1,0:T(8,128)(2,1)S(1)}, u32[]{:S(2)}, u32[]{:S(2)}) collective-permute-start(bf16[256,128]{1,0:T(8,128)(2,1)S(1)} %get-tuple-element.170), channel_id=1, source_target_pairs={{0,96},{32,64},{64,32},{96,0},{1,97},{33,65},{65,33},{97,1},{2,98}... | collective-permute-start | bytes 196616 | tf_op jit(solution)/shard_map/ppermute | solution.py:499
  143.0 7.1 %collective-permute-start.34 = (bf16[16,3712]{1,0:T(8,128)(2,1)S(1)}, bf16[16,3712]{1,0:T(8,128)(2,1)S(1)}, u32[]{:S(2)}, u32[]{:S(2)}) collective-permute-start(bf16[16,3712]{1,0:T(8,128)(2,1)S(1)} %get-tuple-element.172), channel_id=1, source_target_pairs={{0,2},{1,3},{2,0},{3,1},{4,6},{5,7},{6,4},{7,5},{8,10},{9,11},{10,... | collective-permute-start | bytes 356360 | tf_op jit(solution)/shard_map/ppermute | solution.py:499
  144.7 7.0 %collective-permute-start.35 = (bf16[16,3712]{1,0:T(8,128)(2,1)S(1)}, bf16[16,3712]{1,0:T(8,128)(2,1)S(1)}, u32[]{:S(2)}, u32[]{:S(2)}) collective-permute-start(bf16[16,3712]{1,0:T(8,128)(2,1)S(1)} %get-tuple-element.173), channel_id=1, source_target_pairs={{0,3},{1,2},{2,1},{3,0},{4,7},{5,6},{6,5},{7,4},{8,11},{9,10},{10,... | collective-permute-start | bytes 356360 | tf_op jit(solution)/shard_map/ppermute | solution.py:499
  146.1 5.6 %collective-permute-start.33 = (bf16[16,3712]{1,0:T(8,128)(2,1)S(1)}, bf16[16,3712]{1,0:T(8,128)(2,1)S(1)}, u32[]{:S(2)}, u32[]{:S(2)}) collective-permute-start(bf16[16,3712]{1,0:T(8,128)(2,1)S(1)} %get-tuple-element.160), channel_id=1, source_target_pairs={{0,1},{1,0},{2,3},{3,2},{4,5},{5,4},{6,7},{7,6},{8,9},{9,8},{10,11... | collective-permute-start | bytes 356360 | tf_op jit(solution)/shard_map/ppermute | solution.py:499
